TPU v7x, 32 devices: a whole 2x2x4 slice. The times are simulated.
32 devices in a mesh: wide: 8 (over z, x), narrow: 4 (over y, core).
Axes of the slice: x: 2, y: 2, z: 4, core: 2. Of those that a mesh axis runs over, the one named last changes fastest.
Arguments:
- tokens: bfloat16 [32, 512, 1120], P('wide', 'narrow'), may hold values from -6 to 6
- lengths: int32 [32], P('wide'), may hold values from 64 to 512, as said below
- norm1_gain: float32 [1120], replicated, may hold values from 0.1 to 1.9
- norm1_bias: float32 [1120], replicated, may hold values from -3 to 3
- w_qkv: bfloat16 [1120, 3, 1120], replicated, may hold values from -0.25 to 0.25
- w_out: bfloat16 [1120, 1120], replicated, may hold values from -1 to 1
- norm2_gain: float32 [1120], replicated, may hold values from 0.1 to 1.9
- norm2_bias: float32 [1120], replicated, may hold values from -3 to 3
- w_up: bfloat16 [1120, 4480], replicated, may hold values from -0.1875 to 0.1875
- bias_up: float32 [4480], replicated, may hold values from -3 to 3
- w_down: bfloat16 [4480, 1120], replicated, may hold values from -0.09375 to 0.09375
- bias_down: float32 [1120], replicated, may hold values from -3 to 3
- cotangent: bfloat16 [32, 512, 1120], P('wide', 'narrow'), may hold values from -6 to 6
Outputs:
- output: bfloat16 [32, 512, 1120], P('wide', 'narrow')
- input_grad: float32 [32, 512, 1120], P('wide', 'narrow')
- grad_norm1_gain: float32 [1120], P('narrow')
- grad_norm1_bias: float32 [1120], P('narrow')
- grad_w_qkv: float32 [1120, 3, 1120], P(None, None, 'narrow')
- grad_w_out: float32 [1120, 1120], P('narrow')
- grad_norm2_gain: float32 [1120], P('narrow')
- grad_norm2_bias: float32 [1120], P('narrow')
- grad_w_up: float32 [1120, 4480], P(None, 'narrow')
- grad_bias_up: float32 [4480], P('narrow')
- grad_w_down: float32 [4480, 1120], P('narrow')
- grad_bias_down: float32 [1120], P('narrow')
Inputs may be any that keep to these rules, and one draw needn't show every extreme that they name: In every aligned block of 4 cells (the cells of one index of wide) exactly one cell, drawn from the seed, has length 512; in one block, drawn from the seed, another cell has length 64; the other lengths follow a heavy tail and are mostly short.
All inputs are finite; a program needn't handle non-finite values.
Results may differ from a plain program's by a relative error of at most 0.015.
The roundings to bfloat16 on the way count: a program that leaves them out, or rounds other values in their place, can miss the bound.
Values may be sent and summed in bfloat16 or wider, within the bound.
A program may use at most 192 MiB of HBM per device.

v0:
```python
from functools import partial

import jax
import jax.numpy as jnp
from jax import lax
from jax.sharding import PartitionSpec as P

HD = 56


def normalize(values):
    mean_value = jnp.mean(values, axis=-1, keepdims=True)
    centred = values - mean_value
    variance = jnp.mean(centred * centred, axis=-1, keepdims=True)
    inverse = lax.rsqrt(variance + 1e-05)
    return (centred * inverse, inverse)


def norm_back(grad_hat, normed, inverse):
    mean_grad = jnp.mean(grad_hat, axis=-1, keepdims=True)
    mean_cross = jnp.mean(grad_hat * normed, axis=-1, keepdims=True)
    return inverse * (grad_hat - mean_grad - normed * mean_cross)


def split_heads(packed):
    seq_len = packed.shape[0]
    local_heads = packed.shape[2] // HD
    query = packed[:, 0].reshape(seq_len, local_heads, HD)
    keys = packed[:, 1].reshape(seq_len, local_heads, HD)
    values = packed[:, 2].reshape(seq_len, local_heads, HD)
    return (query, keys, values)


def masked_scores(query, keys, length):
    seq_len = query.shape[0]
    positions = jnp.arange(seq_len)
    allowed = (positions[None, :] <= positions[:, None]) & (positions[None, :] < length)
    scores = jnp.einsum("qhe,khe->hqk", query, keys, preferred_element_type=jnp.float32) * HD ** (
        -0.5
    )
    return jnp.where(allowed[None], scores, jnp.float32(-1e30))


def cell_attention(item):
    packed, length = item
    query, keys, values = split_heads(packed)
    scores = masked_scores(query, keys, length)
    peak = jnp.max(scores, axis=-1, keepdims=True)
    expo = jnp.exp(scores - peak)
    total = jnp.sum(expo, axis=-1, keepdims=True)
    probs = (expo / total).astype(jnp.bfloat16)
    mixed = jnp.einsum("hqk,khe->qhe", probs, values, preferred_element_type=jnp.float32)
    log_total = (peak + jnp.log(total))[..., 0]
    return (mixed.reshape(packed.shape[0], -1).astype(jnp.bfloat16), log_total)


def cell_attention_back(item):
    packed, length, log_total, grad_mixed = item
    query, keys, values = split_heads(packed)
    scores = masked_scores(query, keys, length)
    probs = jnp.exp(scores - log_total[..., None])
    grad_heads = grad_mixed.reshape(values.shape)
    grad_values = jnp.einsum(
        "hqk,qhe->khe", probs.astype(jnp.bfloat16), grad_heads, preferred_element_type=jnp.float32
    )
    grad_probs = jnp.einsum("qhe,khe->hqk", grad_heads, values, preferred_element_type=jnp.float32)
    inner = jnp.sum(probs * grad_probs, axis=-1, keepdims=True)
    grad_scores = (probs * (grad_probs - inner) * HD ** (-0.5)).astype(jnp.bfloat16)
    grad_query = jnp.einsum("hqk,khe->qhe", grad_scores, keys, preferred_element_type=jnp.float32)
    grad_keys = jnp.einsum("hqk,qhe->khe", grad_scores, query, preferred_element_type=jnp.float32)
    stacked = jnp.stack([grad_query, grad_keys, grad_values], axis=1)
    return stacked.reshape(packed.shape).astype(jnp.bfloat16)


def on_device(
    tokens,
    lengths,
    norm1_gain,
    norm1_bias,
    w_qkv,
    w_out,
    norm2_gain,
    norm2_bias,
    w_up,
    bias_up,
    w_down,
    bias_down,
    cotangent,
):
    inputs = tokens.astype(jnp.float32)
    normed1, inverse1 = normalize(inputs)
    hidden1 = (normed1 * norm1_gain + norm1_bias).astype(jnp.bfloat16)
    projected = jnp.einsum(
        "cpd,dke->cpke", hidden1, w_qkv, preferred_element_type=jnp.float32
    ).astype(jnp.bfloat16)
    spread = lax.all_to_all(projected, "narrow", split_axis=3, concat_axis=1, tiled=True)
    attended, log_totals = lax.map(cell_attention, (spread, lengths))
    mixed = lax.all_to_all(attended, "narrow", split_axis=1, concat_axis=2, tiled=True)
    after = inputs + jnp.einsum("cpd,de->cpe", mixed, w_out, preferred_element_type=jnp.float32)
    normed2, inverse2 = normalize(after)
    hidden2 = (normed2 * norm2_gain + norm2_bias).astype(jnp.bfloat16)
    upper = jnp.einsum("cpd,df->cpf", hidden2, w_up, preferred_element_type=jnp.float32) + bias_up
    activated, gelu_back = jax.vjp(partial(jax.nn.gelu, approximate=True), upper)
    act_low = activated.astype(jnp.bfloat16)
    output = (
        after
        + jnp.einsum("cpf,fd->cpd", act_low, w_down, preferred_element_type=jnp.float32)
        + bias_down
    ).astype(jnp.bfloat16)
    grad_direct = cotangent.astype(jnp.float32)
    grad_bias_down = jnp.sum(grad_direct, axis=(0, 1))
    grad_act = jnp.einsum("cpd,fd->cpf", cotangent, w_down, preferred_element_type=jnp.float32)
    grad_upper = gelu_back(grad_act)[0].astype(jnp.bfloat16)
    grad_hidden2 = jnp.einsum("cpf,df->cpd", grad_upper, w_up, preferred_element_type=jnp.float32)
    grad_norm2_gain = jnp.sum(grad_hidden2 * normed2, axis=(0, 1))
    grad_norm2_bias = jnp.sum(grad_hidden2, axis=(0, 1))
    grad_after = grad_direct + norm_back(grad_hidden2 * norm2_gain, normed2, inverse2)
    grad_after_low = grad_after.astype(jnp.bfloat16)
    grad_w_out = jnp.einsum(
        "cpd,cpe->de", mixed, grad_after_low, preferred_element_type=jnp.float32
    )
    grad_mixed = jnp.einsum(
        "cpe,de->cpd", grad_after_low, w_out, preferred_element_type=jnp.float32
    ).astype(jnp.bfloat16)
    grad_spread = lax.all_to_all(grad_mixed, "narrow", split_axis=2, concat_axis=1, tiled=True)
    grad_packed = lax.map(cell_attention_back, (spread, lengths, log_totals, grad_spread))
    grad_projected = lax.all_to_all(grad_packed, "narrow", split_axis=1, concat_axis=3, tiled=True)
    grad_hidden1 = jnp.einsum(
        "cpke,dke->cpd", grad_projected, w_qkv, preferred_element_type=jnp.float32
    )
    grad_norm1_gain = jnp.sum(grad_hidden1 * normed1, axis=(0, 1))
    grad_norm1_bias = jnp.sum(grad_hidden1, axis=(0, 1))
    input_grad = grad_after + norm_back(grad_hidden1 * norm1_gain, normed1, inverse1)
    act_columns, upper_columns = (
        lax.all_to_all(act_low, "narrow", split_axis=2, concat_axis=1, tiled=True),
        lax.all_to_all(grad_upper, "narrow", split_axis=2, concat_axis=1, tiled=True),
    )
    up_bias_share = jnp.sum(upper_columns.astype(jnp.float32), axis=(0, 1))
    down_total = jnp.zeros((act_columns.shape[2], w_down.shape[1]), jnp.float32)
    first_rows = lax.all_gather(hidden1, "narrow", axis=1, tiled=True)
    second_rows = lax.all_gather(hidden2, "narrow", axis=1, tiled=True)
    grad_rows = lax.all_gather(cotangent, "narrow", axis=1, tiled=True)
    count = first_rows.shape[1]
    act_rows = lax.slice_in_dim(act_columns, 0, count, axis=1)
    qkv_total = jnp.einsum(
        "cpd,cpke->dke", first_rows, grad_packed, preferred_element_type=jnp.float32
    )
    up_total = jnp.einsum(
        "cpd,cpf->df", second_rows, upper_columns, preferred_element_type=jnp.float32
    )
    down_total = down_total + jnp.einsum(
        "cpf,cpd->fd", act_rows, grad_rows, preferred_element_type=jnp.float32
    )
    gain_one, bias_one, out_share, gain_two, bias_two, down_bias_share = (
        lax.psum_scatter(
            grad_norm1_gain.astype(jnp.bfloat16), "narrow", scatter_dimension=0, tiled=True
        ).astype(jnp.float32),
        lax.psum_scatter(
            grad_norm1_bias.astype(jnp.bfloat16), "narrow", scatter_dimension=0, tiled=True
        ).astype(jnp.float32),
        lax.psum_scatter(
            grad_w_out.astype(jnp.bfloat16), "narrow", scatter_dimension=0, tiled=True
        ).astype(jnp.float32),
        lax.psum_scatter(
            grad_norm2_gain.astype(jnp.bfloat16), "narrow", scatter_dimension=0, tiled=True
        ).astype(jnp.float32),
        lax.psum_scatter(
            grad_norm2_bias.astype(jnp.bfloat16), "narrow", scatter_dimension=0, tiled=True
        ).astype(jnp.float32),
        lax.psum_scatter(
            grad_bias_down.astype(jnp.bfloat16), "narrow", scatter_dimension=0, tiled=True
        ).astype(jnp.float32),
    )
    summed = lax.psum(
        (
            gain_one,
            bias_one,
            qkv_total,
            out_share,
            gain_two,
            bias_two,
            up_total,
            up_bias_share,
            down_total,
            down_bias_share,
        ),
        "wide",
    )
    return (
        output,
        input_grad,
        summed[0],
        summed[1],
        summed[2],
        summed[3],
        summed[4],
        summed[5],
        summed[6],
        summed[7],
        summed[8],
        summed[9],
    )


def solution(mesh):
    in_specs = (
        P("wide", "narrow", None),
        P("wide"),
        P(),
        P(),
        P(),
        P(),
        P(),
        P(),
        P(),
        P(),
        P(),
        P(),
        P("wide", "narrow", None),
    )
    out_specs = (
        P("wide", "narrow", None),
        P("wide", "narrow", None),
        P("narrow"),
        P("narrow"),
        P(None, None, "narrow"),
        P("narrow", None),
        P("narrow"),
        P("narrow"),
        P(None, "narrow"),
        P("narrow"),
        P("narrow", None),
        P("narrow"),
    )
    return jax.shard_map(
        on_device, mesh=mesh, in_specs=in_specs, out_specs=out_specs, check_vma=False
    )
```

profile of v0, /device:TPU:0, one launch (start us, length us, event | category | flops | bytes accessed | tf_op | source)
XLA Modules:
  0.0 967.9 jit_solution(13773890683716826495)
XLA Ops:
  13.8 8.2 fusion.66
  22.0 9.6 copy.79
  31.7 4.7 all-to-all-start
  37.4 63.2 %all-to-all-done = bf16[4,128,3,1120]{1,0,2,3:T(4,128)(2,1)} async-done(((bf16[4,128,3,1120]{1,0,2,3:T(4,128)(2,1)}), bf16[4,128,3,1120]{1,0,2,3:T(4,128)(2,1)}, u32[]{:S(2)}, u32[]{:S(2)}) %all-to-all-start) | async-done | bytes 3440672 | tf_op jit(solution)/shard_map/all_to_all | solution.py:96
  100.6 5.6 copy.80
  106.3 6.9 all_to_all.81
  113.1 29.3 %while.22 = (s32[]{:T(128)}, bf16[4,512,280]{1,2,0:T(8,128)(2,1)}, f32[4,5,512]{2,1,0:T(8,128)S(1)}, bf16[4,512,3,280]{1,3,2,0:T(8,128)(2,1)}, s32[4]{0:T(128)S(1)}, /*index=5*/s32[]{:T(128)}) while((s32[]{:T(128)}, bf16[4,512,280]{1,2,0:T(8,128)(2,1)}, f32[4,5,512]{2,1,0:T(8,128)S(1)}, bf16[4,512,3,280]{1,3,2,0:T(8,128)(2,1)}, ...), condition=%wide.region_5.6_spmd, body=%wide.region_2.5_spmd.sunk | while | flops 309995520 | bytes 22039656 | solution.py:97
  142.5 3.4 copy.81
  145.9 24.5 %all_to_all.108 = bf16[4,512,280]{2,0,1:T(4,128)(2,1)} all-to-all(bf16[4,512,280]{2,0,1:T(4,128)(2,1)} %copy.81), channel_id=1, replica_groups=mesh['wide'=8,'narrow'=4] {'narrow'}, dimensions={1} | all-to-all | bytes 2293760 | tf_op jit(solution)/shard_map/all_to_all | solution.py:98
  170.4 3.6 copy.82
  174.0 3.3 fusion.105
  180.2 15.9 %multiply_convert_fusion.1 = (bf16[4,128,4480]{2,1,0:T(8,128)(2,1)}, f32[4,128,4480]{2,1,0:T(8,128)}) fusion(f32[4480]{0:T(1024)S(1)} %copy-done.23, bf16[4,128,1120]{1,2,0:T(8,128)(2,1)} %add_convert_fusion, bf16[1120,4480]{1,0:T(8,128)(2,1)} %param.25), kind=kOutput, calls=%fused_computation.58 | convolution fusion | flops 5160960000 | bytes 24962560 | tf_op jit(solution)/shard_map/cpd,df->cpf/dot_general | solution.py:102
  196.2 16.6 %fusion.49 = bf16[4,128,4480]{2,1,0:T(8,128)(2,1)S(1)} fusion(f32[4,128,4480]{2,1,0:T(8,128)} %get-tuple-element.131, bf16[4,128,1120]{1,2,0:T(8,128)(2,1)S(1)} %copy-done.7, bf16[4480,1120]{0,1:T(8,128)(2,1)} %param.27), kind=kOutput, calls=%fused_computation.56 | convolution fusion | flops 5183897600 | bytes 24944640 | tf_op jit(solution)/shard_map/cpd,fd->cpf/dot_general | solution.py:112
  212.9 7.0 multiply_reduce_fusion.1
  222.3 5.7 copy.84
  228.1 3.5 all-to-all-start.2
  231.6 8.3 copy.89
  239.9 7.2 all-to-all-done.2
  248.1 5.0 all-to-all-start.4
  253.2 8.5 copy.92
  261.6 4.4 fusion.59
  269.2 50.1 %all-to-all-done.4 = bf16[4,128,4480]{1,0,2:T(4,128)(2,1)} async-done(((bf16[4,128,4480]{1,0,2:T(4,128)(2,1)}), bf16[4,128,4480]{1,0,2:T(4,128)(2,1)}, u32[]{:S(2)}, u32[]{:S(2)}) %all-to-all-start.4) | async-done | bytes 4587552 | tf_op jit(solution)/shard_map/all_to_all | solution.py:136
  319.4 4.9 all-to-all-start.5
  324.3 120.1 %while.23 = (s32[]{:T(128)}, bf16[4,512,3,280]{1,3,2,0:T(8,128)(2,1)}, bf16[4,512,3,280]{1,3,2,0:T(8,128)(2,1)}, s32[4]{0:T(128)S(1)}, f32[4,5,512]{2,1,0:T(8,128)S(1)}, /*index=5*/bf16[4,512,280]{1,2,0:T(8,128)(2,1)}, s32[]{:T(128)}) while((s32[]{:T(128)}, bf16[4,512,3,280]{1,3,2,0:T(8,128)(2,1)}, bf16[4,512,3,280]{1,3,2,0:T(8,128)(2,1)}, ...), condition=%wide.region_12.13_spmd, body=%wide.region_10.12_spmd.sunk | while | flops 755894784 | bytes 66829456 | solution.py:126
  336.1 8.6 fusion.173
  344.7 8.7 fusion.174
  366.1 8.6 fusion.173
  374.7 8.7 fusion.174
  396.1 8.6 fusion.173
  404.7 8.7 fusion.174
  426.1 8.6 fusion.173
  434.7 8.7 fusion.174
  444.4 5.1 copy.90
  449.5 5.0 copy.93
  454.5 9.9 %fusion.69 = f32[1120,3,280]{0,2,1:T(8,128)} fusion(bf16[4,512,3,280]{1,3,2,0:T(8,128)(2,1)} %get-tuple-element.74, bf16[4,512,1120]{1,2,0:T(8,128)(2,1)} %all-gather.4.cloned.1.call-done), kind=kOutput, calls=%fused_computation.75 | convolution fusion | flops 3853516800 | bytes 11791360 | tf_op jit(solution)/shard_map/cpd,cpke->dke/dot_general | solution.py:145
  464.5 10.8 %convolution_bitcast_fusion = f32[1120,1120]{1,0:T(8,128)} fusion(bf16[4,512,1120]{1,2,0:T(8,128)(2,1)} %all-gather.8.cloned.1.call-done, bf16[4,4,140,8,128]{4,3,2,1,0:T(8,128)(2,1)} %bitcast.227), kind=kOutput, calls=%fused_computation.59 | convolution fusion | flops 5138022400 | bytes 14192640 | tf_op jit(solution)/shard_map/cpf,cpd->fd/dot_general | solution.py:151
  475.3 11.0 %convolution_bitcast_fusion.1 = f32[1120,1120]{1,0:T(8,128)} fusion(bf16[4,512,1120]{1,2,0:T(8,128)(2,1)} %all-gather.6.cloned.1.call-done, bf16[4,4,140,8,128]{4,3,2,1,0:T(8,128)(2,1)} %bitcast.214), kind=kOutput, calls=%fused_computation.60 | convolution fusion | flops 5138022400 | bytes 14192640 | tf_op jit(solution)/shard_map/cpd,cpf->df/dot_general | solution.py:148
  486.3 7.8 copy.86
  494.1 5.1 all-to-all-start.3
  502.0 10.4 %fusion.81 = bf16[4,128,1120]{1,2,0:T(8,128)(2,1)} fusion(f32[4,128,1120]{1,2,0:T(8,128)S(1)} %copy-done.5, bf16[4,128,4480]{2,1,0:T(8,128)(2,1)} %get-tuple-element.130, bf16[4480,1120]{0,1:T(8,128)(2,1)} %param.27, f32[1120]{0:T(1024)S(1)} %copy-done.24), kind=kOutput, calls=%fused_computation.82 | convolution fusion | flops 5139742720 | bytes 18067840 | tf_op jit(solution)/shard_map/cpf,fd->cpd/dot_general | solution.py:107
  512.5 40.6 %all-to-all-done.3 = bf16[4,512,3,280]{3,0,2,1:T(4,128)(2,1)} async-done(((bf16[4,512,3,280]{3,0,2,1:T(4,128)(2,1)}), bf16[4,512,3,280]{3,0,2,1:T(4,128)(2,1)}, u32[]{:S(2)}, u32[]{:S(2)}) %all-to-all-start.3) | async-done | bytes 3440672 | tf_op jit(solution)/shard_map/all_to_all | solution.py:127
  553.1 8.3 copy.87
  561.4 10.6 %fusion.98 = (bf16[1120]{0:T(1024)(128)(2,1)S(1)}, f32[4,128]{1,0:T(4,128)S(1)}, f32[4,128]{1,0:T(4,128)S(1)}, bf16[1120]{0:T(1024)(128)(2,1)S(1)}, f32[4,128,1120]{1,2,0:T(8,128)}) fusion(bf16[4,128,1120]{1,2,0:T(8,128)(2,1)S(1)} %copy-done.6, f32[4,128]{1,0:T(4,128)S(1)} %copy-done.19, f32[4,128]{1,0:T(4,128)S(1)} %copy-done.17, f32[1120]{0:T(1024)S(1)} %copy-done.15, ...), kind=kOutput, calls=%fused_computation.98 | convolution fusion | flops 3859248128 | bytes 14424832 | tf_op jit(solution)/shard_map/cpke,dke->cpd/dot_general | solution.py:128
  572.0 11.1 %all-reduce.8 = (bf16[1120]{0:T(1024)(128)(2,1)S(1)}, bf16[1120]{0:T(1024)(128)(2,1)S(1)}, bf16[1120]{0:T(1024)(128)(2,1)S(1)}, bf16[1120]{0:T(1024)(128)(2,1)S(1)}, bf16[1120]{0:T(1024)(128)(2,1)S(1)}) all-reduce(bf16[1120]{0:T(1024)(128)(2,1)S(1)} %get-tuple-element.77, ...), channel_id=2, replica_groups=mesh['wide'=8,'narrow'=4] {'narrow'}, use_global_device_ids=true, to_apply=%region_16.17.clone | all-reduce | flops 5600 | bytes 22400
  586.7 3.8 fusion.97
  590.5 95.5 %all-reduce.13 = (f32[280]{0:T(512)}, f32[280]{0:T(512)}, f32[280,1120]{1,0:T(8,128)}, f32[280]{0:T(512)}, f32[280]{0:T(512)}, /*index=5*/f32[1120]{0:T(1024)}, f32[280]{0:T(512)}) all-reduce(f32[280]{0:T(512)S(1)} %dynamic-slice_convert_fusion.4, ...), channel_id=1, replica_groups=mesh['wide'=8,'narrow'=4] {'wide'}, use_global_device_ids=true, to_apply=%region_17.18 | all-reduce | flops 316120 | bytes 1901760 | tf_op jit(solution)/shard_map/psum | solution.py:174
  685.9 264.3 %all-reduce.12.cloned.1.call-done = (f32[1120,3,280]{0,2,1:T(8,128)}, f32[1120,1120]{1,0:T(8,128)}, f32[1120,1120]{1,0:T(8,128)}) async-done(((f32[1120,3,280]{0,2,1:T(8,128)}, f32[1120,1120]{1,0:T(8,128)}, f32[1120,1120]{1,0:T(8,128)}), (f32[1120,3,280]{0,2,1:T(8,128)}, f32[1120,1120]{1,0:T(8,128)}, f32[1120,1120]{1,0:T(8,128)})) %all-reduce.12.cloned.1.call-update) | async-done | bytes 13798416 | tf_op jit(solution)/shard_map/psum | solution.py:174
  950.2 4.5 copy.147
  (200 shorter events, 108.8 us)
Async XLA Ops:
  7.2 166.8 %copy-start = (bf16[1120,1120]{1,0:T(8,128)(2,1)S(1)}, bf16[1120,1120]{1,0:T(8,128)(2,1)}, u32[]{:S(2)}) copy-start(bf16[1120,1120]{1,0:T(8,128)(2,1)} %param.22) | copy-start | bytes 7526404
  7.2 447.3 %all-gather.4.cloned.1.call-start = ((), (), s32[]{:S(2)}) async-start(), calls=%async_computation.7 | async-start | bytes 5734400 | tf_op jit(solution)/shard_map/all_gather | solution.py:140
  8.8 1.6 copy-start.16
  10.4 0.6 copy-start.18
  31.7 69.0 %all-to-all-start = ((bf16[4,128,3,1120]{1,0,2,3:T(4,128)(2,1)}), bf16[4,128,3,1120]{1,0,2,3:T(4,128)(2,1)}, u32[]{:S(2)}, u32[]{:S(2)}) async-start(bf16[4,128,3,1120]{1,0,2,3:T(4,128)(2,1)} %copy.79), calls=%async_computation | async-start | bytes 6881280 | tf_op jit(solution)/shard_map/all_to_all | solution.py:96
  36.4 428.1 %all-gather.8.cloned.1.call-start = ((), (), s32[]{:S(2)}) async-start(), calls=%async_computation.9 | async-start | bytes 5734400 | tf_op jit(solution)/shard_map/all_gather | solution.py:142
  37.1 438.1 %all-gather.6.cloned.1.call-start = ((), (), s32[]{:S(2)}) async-start(), calls=%async_computation.8 | async-start | bytes 5734400 | tf_op jit(solution)/shard_map/all_gather | solution.py:141
  106.3 6.9 copy-start.25
  174.0 4.7 copy-start.14
  174.0 4.7 copy-start.20
  177.3 1.4 copy-start.3
  177.3 2.9 copy-start.23
  180.2 16.0 %copy-start.7 = (bf16[4,128,1120]{1,2,0:T(8,128)(2,1)S(1)}, bf16[4,128,1120]{1,2,0:T(8,128)(2,1)}, u32[]{:S(2)}) copy-start(bf16[4,128,1120]{1,2,0:T(8,128)(2,1)} %param.29) | copy-start | bytes 3440644
  180.2 32.6 %slice-start.2 = ((s8[10035200]{0:T(1024)(128)(4,1)}), s8[4194304]{0:T(1024)(128)(4,1)S(1)}, s32[]{:S(2)}) async-start(s8[10035200]{0:T(1024)(128)(4,1)} %bitcast.232), calls=%async_computation.14 | async-start | bytes 8388608
  196.2 16.7 %copy-start.4 = (f32[4,128,1120]{1,2,0:T(8,128)S(1)}, f32[4,128,1120]{1,2,0:T(8,128)}, u32[]{:S(2)}) copy-start(f32[4,128,1120]{1,2,0:T(8,128)} %copy-done.3) | copy-start | bytes 6881284
  196.2 16.7 %slice-start.3 = ((s8[10035200]{0:T(1024)(128)(4,1)}), s8[4194304]{0:T(1024)(128)(4,1)S(1)}, s32[]{:S(2)}) async-start(s8[10035200]{0:T(1024)(128)(4,1)} %bitcast.232), calls=%async_computation.15 | async-start | bytes 8388608
  196.2 16.7 %slice-start.4 = ((s8[10035200]{0:T(1024)(128)(4,1)}), s8[1646592]{0:T(1024)(128)(4,1)S(1)}, s32[]{:S(2)}) async-start(s8[10035200]{0:T(1024)(128)(4,1)} %bitcast.232), calls=%async_computation.16 | async-start | bytes 3293184
  212.9 7.0 copy-start.11
  220.6 1.7 copy-start.8
  228.1 19.0 %all-to-all-start.2 = ((bf16[4,128,1120]{1,0,2:T(4,128)(2,1)}), bf16[4,128,1120]{1,0,2:T(4,128)(2,1)S(1)}, u32[]{:S(2)}, u32[]{:S(2)}) async-start(bf16[4,128,1120]{1,0,2:T(4,128)(2,1)} %copy.84), calls=%async_computation.2 | async-start | bytes 2293760 | tf_op jit(solution)/shard_map/all_to_all | solution.py:125
  247.1 1.0 copy-start.12
  248.1 71.3 %all-to-all-start.4 = ((bf16[4,128,4480]{1,0,2:T(4,128)(2,1)}), bf16[4,128,4480]{1,0,2:T(4,128)(2,1)}, u32[]{:S(2)}, u32[]{:S(2)}) async-start(bf16[4,128,4480]{1,0,2:T(4,128)(2,1)} %copy.89), calls=%async_computation.4 | async-start | bytes 9175040 | tf_op jit(solution)/shard_map/all_to_all | solution.py:136
  253.1 337.4 %reduce-scatter.4.cloned.1.call-start = ((), (), s32[]{:S(2)}) async-start(), calls=%async_computation.10 | async-start | bytes 3225600
  253.2 8.5 copy-start.9
  319.4 130.1 %all-to-all-start.5 = ((bf16[4,128,4480]{1,0,2:T(4,128)(2,1)}), bf16[4,128,4480]{1,0,2:T(4,128)(2,1)}, u32[]{:S(2)}, u32[]{:S(2)}) async-start(bf16[4,128,4480]{1,0,2:T(4,128)(2,1)} %copy.92), calls=%async_computation.5 | async-start | bytes 9175040 | tf_op jit(solution)/shard_map/all_to_all | solution.py:135
  324.3 625.9 %all-reduce.12.cloned.1.call-start = ((), (), s32[]{:S(2)}) async-start(), calls=%async_computation.11 | async-start | bytes 28385280 | tf_op jit(solution)/shard_map/psum | solution.py:174
  329.6 2.3 copy-start.2
  359.7 2.3 copy-start.2
  389.7 2.3 copy-start.2
  419.7 2.3 copy-start.2
  494.1 6.6 copy-start.26
  494.1 7.9 copy-start.5
  494.1 7.9 copy-start.24
  494.1 58.9 %all-to-all-start.3 = ((bf16[4,512,3,280]{3,0,2,1:T(4,128)(2,1)}), bf16[4,512,3,280]{3,0,2,1:T(4,128)(2,1)}, u32[]{:S(2)}, u32[]{:S(2)}) async-start(bf16[4,512,3,280]{3,0,2,1:T(4,128)(2,1)} %copy.86), calls=%async_computation.3 | async-start | bytes 9437184 | tf_op jit(solution)/shard_map/all_to_all | solution.py:127
  553.1 8.3 copy-start.6
  553.1 8.3 copy-start.15
  553.1 8.3 copy-start.17
  553.1 8.3 copy-start.19
  561.4 10.6 %copy-start.21 = (bf16[1120]{0:T(1024)(128)(2,1)S(1)}, bf16[1120]{0:T(1024)(128)(2,1)}, u32[]{:S(2)}) copy-start(bf16[1120]{0:T(1024)(128)(2,1)} %get-tuple-element.75) | copy-start | bytes 6724
  561.4 10.6 %copy-start.22 = (bf16[1120]{0:T(1024)(128)(2,1)S(1)}, bf16[1120]{0:T(1024)(128)(2,1)}, u32[]{:S(2)}) copy-start(bf16[1120]{0:T(1024)(128)(2,1)} %get-tuple-element.81) | copy-start | bytes 6724
  583.0 3.7 copy-start.13
  950.2 4.5 copy-start.10
  950.2 8.2 slice-start
  954.7 3.9 slice-start.1
  954.7 6.3 copy-start.1
Sparse Core Ops, SparseCore 0:
  13.9 51.4 all-gather.3
  67.0 48.3 all-gather.7
  180.3 37.1 all-gather.5
  266.2 49.7 reduce-scatter.3
  486.4 463.7 all-reduce.11
where the time goes:
time: 977 us; the launch traced here: 968 us
  waiting for transfers between devices  426 us (44%)
  matrix products  213 us (22%)
  blocking collectives  131 us (13%)
  local copies, waits for them, and re-layouts  126 us (13%)
  other arithmetic  32 us (3%)
  starting transfers between devices  23.7 us (2%)
  between operations  15.2 us (2%)
    psum x1, waiting for transfers between devices, on_device(): lax.psum((gain_one, bias_one, qkv_total, out_share, gain_two, bias_two, u...  264 us
    psum x1, blocking collectives, on_device(): lax.psum((gain_one, bias_one, qkv_total, out_share, gain_two, bias_two, u...  95.5 us
    all_to_all x1, waiting for transfers between devices, on_device(): lax.all_to_all(projected, 'narrow', split_axis=3, concat_axis=1, tiled=True)  63.2 us
    all_to_all x1, waiting for transfers between devices, on_device(): lax.all_to_all(grad_upper, 'narrow', split_axis=2, concat_axis=1, tiled=T...  50.1 us
    all_to_all x1, waiting for transfers between devices, on_device(): lax.all_to_all(grad_packed, 'narrow', split_axis=1, concat_axis=3, tiled=...  40.6 us
    dot_general x4, matrix products, cell_attention_back(): jnp.einsum('hqk,khe->qhe', grad_scores, keys, preferred_element_type=jnp....  34.9 us
    dot_general x4, matrix products, cell_attention_back(): jnp.einsum('hqk,qhe->khe', grad_scores, query, preferred_element_type=jnp...  34.4 us
    all_to_all x1, blocking collectives, on_device(): lax.all_to_all(attended, 'narrow', split_axis=1, concat_axis=2, tiled=True)  24.5 us
  transfers between devices with their start and end apart: 10, of which 5 were waited for; matrix products, arithmetic and copies ran while one was open for 35% of the time, Pallas kernels for 0%

commit v1 on v0

v1 whole, which is shorter than its diff:
```python
import functools
import types

import jax
import jax.numpy as jnp
from jax import lax
from jax.experimental import pallas as pl
from jax.experimental.pallas import tpu as pltpu
from jax.sharding import PartitionSpec as P

HD = 56
SCALE = HD**-0.5
F32, BF16 = jnp.float32, jnp.bfloat16
MESH = pl.DeviceIdType.MESH
VMEM_LIMIT = 62 * 1024 * 1024
LINE, PAIR = 4, 2
BLOCK = LINE * PAIR
SLOTS, STATES, STATES_A = 4, 11, 8
CORE, CY, CA, CB, CC, CX, AX, AY, A1, A2, A3, AG, GATHER = range(13)
CHANNELS = GATHER + 6


def dot(a, b, dims):
    return lax.dot_general(a, b, (dims, ((), ())), preferred_element_type=F32)


NN, NT, TN = ((1,), (0,)), ((1,), (1,)), ((0,), (0,))


def head_mask(h, start, size):
    lane = start + lax.broadcasted_iota(jnp.int32, (1, size), 1)
    return (lane >= h * HD) & (lane < h * HD + HD)


class Reducer:
    hops = 9

    def __init__(self, rows_c, rows_a, width):
        self.rows_c, self.rows_a, self.width = rows_c, rows_a, width
        self.rows = rows_c + rows_a
        self.shard, self.half = rows_c // LINE, rows_a // 2

    def scratch(self):
        c, a, q, h, d = self.rows_c, self.rows_a, self.shard, self.half, self.width
        buffers = dict(
            own=(2, self.rows, d),
            core_in=(SLOTS, 2, self.rows, d),
            cy_out=(2, c, d),
            cy_in=(SLOTS, c, d),
            c_state=(STATES, c, d),
            ca_in=(SLOTS, 3 * q, d),
            cb_in=(SLOTS, 2 * q, d),
            cc_in=(SLOTS, q, d),
            cx_in=(SLOTS, q, d),
            ax_out=(2, 2, h, d),
            ax_keep=(2, 2, h, d),
            ax_in=(SLOTS, 2, h, d),
            ay_out=(2, h, d),
            ay_in=(SLOTS, h, d),
            a_sum=(4, h, d),
            a1_in=(SLOTS, h, d),
            a2_in=(SLOTS, h, d),
            a_state=(STATES_A, 2, h, d),
        )
        result = {name: pltpu.VMEM(shape, BF16) for name, shape in buffers.items()}
        result.update(
            net_send=pltpu.SemaphoreType.DMA((CHANNELS, SLOTS)),
            net_recv=pltpu.SemaphoreType.DMA((CHANNELS, SLOTS)),
            load=pltpu.SemaphoreType.DMA((2,)),
            c_store=pltpu.SemaphoreType.DMA((2,)),
            a_store=pltpu.SemaphoreType.DMA((2,)),
        )
        return result

    def bind(self, part_ref, out_ref, refs):
        self.part_ref, self.out_ref, self.refs = part_ref, out_ref, refs
        wide, narrow = lax.axis_index("wide"), lax.axis_index("narrow")
        self.wide, self.narrow = wide, narrow
        self.z, self.x = lax.rem(wide, BLOCK) // PAIR, lax.rem(wide, PAIR)
        self.y, self.core = narrow // 2, lax.rem(narrow, 2)
        flip = lambda index, bit: index + 1 - 2 * bit
        self.at_core = (wide, flip(narrow, self.core))
        self.at_y = (wide, narrow + 2 - 4 * self.y)
        self.at_cross = (wide, flip(narrow, self.core) + 2 - 4 * self.y)
        self.at_x = (flip(wide, self.x), narrow)
        self.at_up = (wide + PAIR, narrow)
        self.at_down = (wide - PAIR, narrow)
        self.rounds = out_ref.shape[0] // self.rows

    def barrier(self):
        z = self.z
        barrier = pltpu.get_barrier_semaphore()

        def greet(target):
            pl.semaphore_signal(barrier, inc=1, device_id=target, device_id_type=MESH)

        for target in (self.at_core, self.at_y, self.at_cross, self.at_x):
            greet(target)
        pl.when(z < LINE - 1)(lambda: greet(self.at_up))
        pl.when(z > 0)(lambda: greet(self.at_down))
        edge = (z == 0) | (z == LINE - 1)
        pl.when(edge)(lambda: pl.semaphore_wait(barrier, 5))
        pl.when(~edge)(lambda: pl.semaphore_wait(barrier, 6))

    def copy(self, channel, k, source, target, device):
        slot = lax.rem(k, SLOTS)
        return pltpu.make_async_remote_copy(
            src_ref=source,
            dst_ref=target,
            send_sem=self.refs.net_send.at[channel, slot],
            recv_sem=self.refs.net_recv.at[channel, slot],
            device_id=device,
            device_id_type=MESH,
        )


    def load(self, k):
        r = self.refs
        return pltpu.make_async_copy(
            self.part_ref.at[:, self.core, pl.ds(k * self.rows, self.rows)],
            r.own,
            r.load.at[lax.rem(k, 2)],
        )

    def core_hop(self, k):
        return self.copy(
            CORE,
            k,
            self.part_ref.at[:, 1 - self.core, pl.ds(k * self.rows, self.rows)],
            self.refs.core_in.at[lax.rem(k, SLOTS)],
            self.at_core,
        )

    def slotted(self, channel, k, source, device):
        r = self.refs
        arrivals = {CY: r.cy_in, CA: r.ca_in, CB: r.cb_in, CC: r.cc_in, CX: r.cx_in}
        arrivals.update({AX: r.ax_in, AY: r.ay_in, A1: r.a1_in, A2: r.a2_in})
        return self.copy(channel, k, source, arrivals[channel].at[lax.rem(k, SLOTS)], device)

    def c_rows(self, k, first, count):
        return self.refs.c_state.at[
            lax.rem(k, STATES), pl.ds(pl.multiple_of(first * self.shard, self.shard), count * self.shard)
        ]

    def line_hops(self, k):
        z, up, down = self.z, self.at_up, self.at_down
        hops = []
        for name, count, up_from in ((CA, 3, 0), (CB, 2, 1), (CC, 1, 2)):
            down_from = LINE - 1 - up_from
            hops.append(
                (
                    name,
                    [
                        (z == up_from, self.slotted(name, k, self.c_rows(k, LINE - count, count), up)),
                        (z == down_from, self.slotted(name, k, self.c_rows(k, 0, count), down)),
                    ],
                    [(z == up_from + 1, LINE - count), (z == down_from - 1, 0)],
                    count,
                )
            )
        return hops

    def gather_hops(self, k, distance):
        z = self.z
        channel = GATHER + 2 * distance
        low, high = jnp.maximum(z - distance, 0), jnp.minimum(z + distance, LINE - 1)
        return [
            (
                (z >= distance) & (z < LINE - 1),
                self.copy(channel, k, self.c_rows(k, low, 1), self.c_rows(k, low, 1), self.at_up),
                z >= distance + 1,
            ),
            (
                (z <= LINE - 1 - distance) & (z > 0),
                self.copy(channel + 1, k, self.c_rows(k, high, 1), self.c_rows(k, high, 1), self.at_down),
                z <= LINE - 2 - distance,
            ),
        ]

    def sum_hops(self, k):
        z, slot = self.z, lax.rem(k, 4)
        own = self.refs.a_sum.at[slot]
        final = self.refs.a_state.at[lax.rem(k, STATES_A), self.x]
        return {
            A1: [
                (z == 0, self.slotted(A1, k, own, self.at_up)),
                (z == LINE - 1, self.slotted(A1, k, own, self.at_down)),
            ],
            A2: [
                (z == 1, self.slotted(A2, k, own, self.at_up)),
                (z == 2, self.slotted(A2, k, own, self.at_down)),
            ],
            A3: [
                (z == 1, self.copy(A3, k, final, final, self.at_down)),
                (z == 2, self.copy(A3, k, final, final, self.at_up)),
            ],
        }

    def store(self, k):
        r, slot, two = self.refs, lax.rem(k, STATES), lax.rem(k, 2)
        base = k * self.rows
        yield pltpu.make_async_copy(
            r.c_state.at[slot], self.out_ref.at[pl.ds(base, self.rows_c)], r.c_store.at[two]
        )

    def store_a(self, k):
        r, slot, two = self.refs, lax.rem(k, STATES_A), lax.rem(k, 2)
        base = k * self.rows + self.rows_c
        for i in range(2):
            yield pltpu.make_async_copy(
                r.a_state.at[slot, i],
                self.out_ref.at[pl.ds(base + i * self.half, self.half)],
                r.a_store.at[two],
            )

    def step(self, t):
        r, c, h, q = self.refs, self.rows_c, self.half, self.shard
        x, y, z = self.x, self.y, self.z

        def stage(delay, body):
            k = t - delay
            pl.when((k >= 0) & (k < self.rounds))(lambda: body(k))

        def start_if(pairs):
            for condition, copy in pairs:
                pl.when(condition)(copy.start)

        def send_wait_if(pairs):
            for condition, copy in pairs:
                pl.when(condition)(copy.wait_send)

        def begin(k):
            self.core_hop(k).start()
            pl.when(k == 0)(self.load(k).start)

        stage(0, begin)

        def after_core(k):
            two, four = lax.rem(k, 2), lax.rem(k, SLOTS)
            copy = self.core_hop(k)
            copy.wait()
            self.load(k).wait()
            total = lambda i, rows: r.own[i, rows] + r.core_in[four, i, rows]
            everything = pl.ds(0, c)
            r.cy_out[two] = total(1 - y, everything)
            self.cy_hop(k).start()
            for i in range(2):
                rows = pl.ds(pl.multiple_of(c + (1 - x) * h, 16), h)
                r.ax_out[two, i] = total(i, rows)
            self.ax_hop(k).start()
            r.c_state[lax.rem(k, STATES), :] = total(y, everything)
            for i in range(2):
                rows = pl.ds(pl.multiple_of(c + x * h, 16), h)
                r.ax_keep[two, i] = total(i, rows)
            pl.when(k + 1 < self.rounds)(lambda: self.load(k + 1).start())

        stage(1, after_core)

        def second(k):
            two, four, slot = lax.rem(k, 2), lax.rem(k, SLOTS), lax.rem(k, STATES)
            self.cy_hop(k).wait()
            r.c_state[slot] = r.c_state[slot] + r.cy_in[four]
            start_if(self.line_hops(k)[0][1])
            self.ax_hop(k).wait()
            r.ay_out[two] = r.ax_keep[two, 1 - y] + r.ax_in[four, 1 - y]
            self.ay_hop(k).start()
            r.a_sum[lax.rem(k, 4)] = r.ax_keep[two, y] + r.ax_in[four, y]

        stage(2, second)

        def line_step(k, hop):
            name, sends, receives, count = self.line_hops(k)[hop]
            four = lax.rem(k, SLOTS)
            send_wait_if(sends)
            for condition, first in receives:

                @pl.when(condition)
                def _(first=first):
                    sends[0][1].wait_recv()
                    rows = self.c_rows(k, first, count)
                    arrived = (r.ca_in, r.cb_in, r.cc_in)[hop]
                    rows[...] = rows[...] + arrived[four]

            if hop < 2:
                start_if(self.line_hops(k)[hop + 1][1])

        def third(k):
            line_step(k, 0)
            four = lax.rem(k, SLOTS)
            self.ay_hop(k).wait()
            r.a_sum[lax.rem(k, 4)] = r.a_sum[lax.rem(k, 4)] + r.ay_in[four]
            start_if(self.sum_hops(k)[A1])

        stage(3, third)

        def fourth(k):
            line_step(k, 1)
            four, slot = lax.rem(k, SLOTS), lax.rem(k, 4)
            hops = self.sum_hops(k)
            send_wait_if(hops[A1])

            @pl.when((z > 0) & (z < LINE - 1))
            def _():
                hops[A1][0][1].wait_recv()
                r.a_sum[slot] = r.a_sum[slot] + r.a1_in[four]

            start_if(hops[A2])

        stage(4, fourth)

        def fifth(k):
            line_step(k, 2)
            self.cx_hop(k).start()
            four, slot = lax.rem(k, SLOTS), lax.rem(k, 4)
            hops = self.sum_hops(k)
            send_wait_if(hops[A2])

            @pl.when((z > 0) & (z < LINE - 1))
            def _():
                hops[A2][0][1].wait_recv()
                r.a_state[lax.rem(k, STATES_A), x] = r.a_sum[slot] + r.a2_in[four]

            start_if(hops[A3])

        stage(5, fifth)

        def sixth(k):
            four = lax.rem(k, SLOTS)
            hops = self.sum_hops(k)
            send_wait_if(hops[A3])
            pl.when((z == 0) | (z == LINE - 1))(lambda: hops[A3][0][1].wait_recv())
            self.ag_hop(k).start()
            self.cx_hop(k).wait()
            rows = self.c_rows(k, z, 1)
            rows[...] = rows[...] + r.cx_in[four]
            for sends, copy, _ in self.gather_hops(k, 0):
                pl.when(sends)(copy.start)

        stage(6, sixth)

        def gather_step(k, distance):
            for sends, copy, receives in self.gather_hops(k, distance):
                pl.when(sends)(copy.wait_send)
                pl.when(receives)(copy.wait_recv)
            if distance < 2:
                for sends, copy, _ in self.gather_hops(k, distance + 1):
                    pl.when(sends)(copy.start)

        def seventh(k):
            gather_step(k, 0)
            self.ag_hop(k).wait()
            for copy in self.store_a(k):
                copy.start()

        stage(7, seventh)

        def eighth(k):
            gather_step(k, 1)
            for copy in self.store_a(k):
                copy.wait()

        stage(8, eighth)

        def ninth(k):
            gather_step(k, 2)
            for copy in self.store(k):
                copy.start()

        stage(9, ninth)

        def tenth(k):
            for copy in self.store(k):
                copy.wait()

        stage(10, tenth)

    def cy_hop(self, k):
        return self.slotted(CY, k, self.refs.cy_out.at[lax.rem(k, 2)], self.at_y)

    def ax_hop(self, k):
        return self.slotted(AX, k, self.refs.ax_out.at[lax.rem(k, 2)], self.at_x)

    def ay_hop(self, k):
        return self.slotted(AY, k, self.refs.ay_out.at[lax.rem(k, 2)], self.at_y)

    def cx_hop(self, k):
        return self.slotted(CX, k, self.c_rows(k, self.z, 1), self.at_x)

    def ag_hop(self, k):
        final = self.refs.a_state.at[lax.rem(k, STATES_A), self.x]
        return self.copy(AG, k, final, final, self.at_x)


class VectorSum:
    def __init__(self, reducer, value, arrived, send, recv):
        self.value, self.arrived, self.send, self.recv = value, arrived, send, recv
        self.net = reducer

    def hop(self, index, device):
        return pltpu.make_async_remote_copy(
            src_ref=self.value,
            dst_ref=self.arrived.at[index],
            send_sem=self.send.at[index],
            recv_sem=self.recv.at[index],
            device_id=device,
            device_id_type=MESH,
        )

    def exchange(self, index):
        return self.hop(index, (self.net.at_core, self.net.at_y, self.net.at_x)[index])

    def step(self, at):
        z, value, arrived = self.net.z, self.value, self.arrived
        middle = (z > 0) & (z < LINE - 1)
        sends = {
            3: ((z == 0, self.net.at_up), (z == LINE - 1, self.net.at_down)),
            4: ((z == 1, self.net.at_up), (z == 2, self.net.at_down)),
            5: ((z == 1, self.net.at_down), (z == 2, self.net.at_up)),
        }

        def start(index):
            for condition, device in sends[index]:
                pl.when(condition)(self.hop(index, device).start)

        def finish(index, receives, add):
            for condition, device in sends[index]:
                pl.when(condition)(self.hop(index, device).wait_send)

            @pl.when(receives)
            def _():
                self.hop(index, sends[index][0][1]).wait_recv()
                value[...] = arrived[index] + value[...] if add else arrived[index]

        def first():
            self.exchange(0).start()

        def pair(index):
            self.exchange(index).wait()
            value[...] = value[...] + arrived[index]
            if index < 2:
                self.exchange(index + 1).start()
            else:
                start(3)

        def outer():
            finish(3, middle, True)
            start(4)

        def inner():
            finish(4, middle, True)
            start(5)

        pl.when(at == 0)(first)
        for index in range(3):
            pl.when(at == index + 1)(functools.partial(pair, index))
        pl.when(at == 4)(outer)
        pl.when(at == 5)(inner)
        pl.when(at == 6)(lambda: finish(5, (z == 0) | (z == LINE - 1), False))


LANES = 128
PARTS = 4
WIDE = 1152


def gelu_both(u):
    c0, c1 = 0.7978845608028654, 0.044715
    square = u * u
    t = jnp.tanh(c0 * u * (1.0 + c1 * square))
    half = 0.5 + 0.5 * t
    slope = half + (0.5 * c0) * u * (1.0 - t * t) * (1.0 + (3.0 * c1) * square)
    return u * half, slope


def norm_rows(values):
    centred = values - jnp.mean(values, axis=-1, keepdims=True)
    inverse = lax.rsqrt(jnp.mean(centred * centred, axis=-1, keepdims=True) + 1e-05)
    return centred * inverse, inverse


def norm_rows_back(grad_hat, normed, inverse):
    mean_grad = jnp.mean(grad_hat, axis=-1, keepdims=True)
    mean_cross = jnp.mean(grad_hat * normed, axis=-1, keepdims=True)
    return inverse * (grad_hat - mean_grad - normed * mean_cross)


def column_sum(values):
    return jnp.sum(values, axis=0, keepdims=True)


def block(i, count):
    return pl.ds(pl.multiple_of(i * count, count), count)


def identity(size):
    row = lax.broadcasted_iota(jnp.int32, (size, size), 0)
    column = lax.broadcasted_iota(jnp.int32, (size, size), 1)
    return jnp.where(row == column, 1.0, 0.0).astype(BF16)


def turned(eye, rows):
    width = rows.shape[1]
    pieces = []
    for at in range(0, width, LANES):
        size = min(LANES, width - at)
        pieces.append(dot(eye[:size, :size], rows[:, at : at + size], NT))
    return jnp.concatenate(pieces, axis=0)


def leftover_rows(tiles):
    first, second, third = tiles
    return [
        [first[:96]],
        [second[:64], first[96:]],
        [third[:32], second[64:]],
        [third[32:]],
    ]


def layer_kernel(reducer, names, *refs):
    r = types.SimpleNamespace(**dict(zip(names, refs)))
    width, part_rows = r.tokens.shape[1:]
    seq = PARTS * part_rows
    feat, ff = width // PARTS, r.w_up.shape[1] // PARTS
    main = ff // LANES
    left = ff - main * LANES
    stride = (r.w_up.shape[1] // LANES - main) // (PARTS - 1)
    heads, group = width // HD, 5
    reducer.bind(r.parts, r.total, r)
    narrow, y = reducer.narrow, reducer.y
    gain1, bias1, gain2, bias2, bias_down = (
        ref[...].reshape(1, width) for ref in (r.gain1, r.bias1, r.gain2, r.bias2, r.bias_down)
    )
    eye = identity(LANES)
    vec = r.vec
    vector_sum = VectorSum(reducer, vec, r.vec_in, r.vec_send, r.vec_recv)

    def local(index, source, target):
        return pltpu.make_async_copy(source, target, r.local.at[index])

    def spread(j, source, target):
        remote = [
            pltpu.make_async_remote_copy(
                src_ref=source.at[device[1]],
                dst_ref=target.at[narrow],
                send_sem=r.spread_send.at[j, d],
                recv_sem=r.spread_recv.at[j, d],
                device_id=device,
                device_id_type=MESH,
            )
            for d, device in enumerate((reducer.at_core, reducer.at_y, reducer.at_cross))
        ]
        return remote, local(j, source.at[narrow], target.at[narrow])

    def weights(i, tiles):
        two = lax.rem(i, 2)
        return [
            pltpu.make_async_copy(
                source.at[:, pl.ds(pl.multiple_of(tile * LANES, LANES), LANES)],
                target.at[two, :, pl.ds(q * LANES, LANES)],
                r.w_load.at[two, n, q],
            )
            for n, (source, target) in enumerate(((r.w_up, r.w_up_in), (r.w_down, r.w_down_in)))
            for q, tile in enumerate(tiles)
        ]

    main_tiles = lambda i: [i + stride * q for q in range(PARTS)]
    left_tiles = [main + stride * q for q in range(PARTS - 1)]

    squares = [local(4 + j, r.w_qkv.at[j], r.square.at[j]) for j in range(3)]
    for copy in squares:
        copy.start()
    reducer.barrier()
    tokens, tokens_own = spread(0, r.tokens, r.x_in)
    cots, cots_own = spread(1, r.cot, r.c_in)
    for copy in tokens + [tokens_own]:
        copy.start()
    for copy in weights(0, main_tiles(0)):
        copy.start()
    vec[...] = jnp.zeros_like(vec)
    for target in (r.q, r.k, r.v, r.m, r.g):
        target[:, width:] = jnp.zeros((seq, WIDE - width), BF16)
    r.acc[...] = jnp.zeros_like(r.acc)
    row = lax.broadcasted_iota(jnp.int32, (seq, seq), 0)
    column = lax.broadcasted_iota(jnp.int32, (seq, seq), 1)
    length = r.lengths[narrow]
    r.bias[...] = jnp.where((column <= row) & (column < length), 0.0, -1e30)
    r.up_bias[...] = r.bias_up[...].reshape(r.up_bias.shape)

    def first_norm(i):
        rows = block(i, part_rows)
        x = dot(eye, r.x_in[i], NT)
        r.x[rows] = x.astype(BF16)
        normed, _ = norm_rows(x)
        r.h[rows] = (normed * gain1 + bias1).astype(BF16)

    def project(side):
        rows = block(side, seq // 2)
        for j, target in enumerate((r.q, r.k, r.v)):
            target[rows, :width] = dot(r.h[rows], r.square[j], NN).astype(BF16)

    tokens_own.wait()
    first_norm(narrow)
    tokens[0].wait()
    first_norm(tokens_peer(reducer, 0))
    for copy in squares:
        copy.wait()
    project(y)
    for d in (1, 2):
        tokens[d].wait()
        first_norm(tokens_peer(reducer, d))
    for copy in cots + [cots_own]:
        copy.start()
    project(1 - y)
    w_out = local(4, r.w_out, r.square.at[0])
    w_out.start()

    def head_at(h):
        return pl.multiple_of(jnp.minimum(h * HD // LANES * LANES, WIDE - 256), LANES)

    def forward(i, carry):
        pair = [(h, head_at(h)) for h in (2 * i, 2 * i + 1)]
        attend_heads(pair, r.q, r.k, r.v, r.m, r.bias)
        return carry

    lax.fori_loop(0, heads // 2, forward, 0)
    w_out.wait()

    def second_norm(i, carry):
        rows = block(i, part_rows)
        after = r.x[rows].astype(F32) + dot(r.m[rows, :width], r.square[0], NN)
        r.rows[rows] = after
        normed, _ = norm_rows(after)
        r.h[rows] = (normed * gain2 + bias2).astype(BF16)
        return carry

    lax.fori_loop(0, PARTS, second_norm, 0)
    for copy in cots + [cots_own]:
        copy.wait()
    for i in range(PARTS):
        r.grad[block(i, part_rows)] = dot(eye, r.c_in[i], NT).astype(BF16)

    upper = pl.ds(0, seq)
    lower = pl.ds(seq, seq)

    def put(count, base):
        return [
            local(
                8 + q,
                r.stage.at[pl.ds(2 * LANES * q, count)],
                r.parts.at[q // 2, q % 2, pl.ds(base, count)],
            )
            for q in range(PARTS)
        ]

    def put_block(i):
        return put(2 * LANES, pl.multiple_of(i * 2 * LANES, 2 * LANES))

    def feed_forward(i, tiles):
        two, count = lax.rem(i, 2), LANES * len(tiles)
        up, down = r.w_up_in[two, :, :count], r.w_down_in[two, :, :count]
        at = [pl.ds(pl.multiple_of(tile * LANES, LANES), LANES) for tile in tiles]
        bias = jnp.concatenate([r.up_bias[:, lanes] for lanes in at], axis=1)
        hidden, cot = r.h[...], r.grad[...]
        act, slope = gelu_both(dot(hidden, up, NN) + bias)
        act = act.astype(BF16)
        grad_up = (dot(cot, down, NN) * slope).astype(BF16)
        r.acc[upper, :width] += dot(act, down, NT)
        r.acc[lower, :width] += dot(grad_up, up, NT)
        total = column_sum(grad_up.astype(F32))
        for q, lanes in enumerate(at):
            vec[0:1, lanes] = total[:, LANES * q : LANES * (q + 1)]
        return dot(act, cot, TN).astype(BF16), dot(grad_up, hidden, TN).astype(BF16)

    def ff_block(i, carry):
        for copy in weights(i, main_tiles(i)):
            copy.wait()

        @pl.when(i + 1 < main)
        def _():
            for copy in weights(i + 1, main_tiles(i + 1)):
                copy.start()

        @pl.when(i + 1 == main)
        def _():
            for copy in weights(main, left_tiles):
                copy.start()

        values = feed_forward(i, main_tiles(i))

        @pl.when(i > 1)
        def _():
            for copy in put_block(i - 1):
                copy.wait()

        for j, value in enumerate(values):
            for q in range(PARTS):
                r.stage[LANES * (2 * q + j) : LANES * (2 * q + j + 1)] = value[
                    LANES * q : LANES * (q + 1)
                ]
        for copy in put_block(i):
            copy.start()
        return carry

    ff_block(0, 0)
    for copy in put_block(0):
        copy.wait()
    reducer.step(jnp.int32(0))

    def ff_step(s, carry):
        lax.fori_loop(2 * s - 1, 2 * s + 1, ff_block, 0)
        reducer.step(s)
        return carry

    ff_steps = main // 2
    lax.fori_loop(1, ff_steps, ff_step, 0)
    lax.fori_loop(main - 1, main, ff_block, 0)
    for copy in weights(main, left_tiles):
        copy.wait()
    values = feed_forward(main, left_tiles)
    for copy in put_block(main - 1):
        copy.wait()
    for j, value in enumerate(values):
        tiles = [value[LANES * q : LANES * (q + 1)] for q in range(PARTS - 1)]
        for q, pieces in enumerate(leftover_rows(tiles)):
            at = 2 * LANES * q + left * j
            for piece in pieces:
                r.stage[at : at + piece.shape[0]] = piece
                at += piece.shape[0]
    put_left = put(2 * left, 2 * LANES * main)
    for copy in put_left:
        copy.start()
    reducer.step(jnp.int32(ff_steps))
    done = ff_steps + 1
    for copy in put_left:
        copy.wait()

    def add_vector(index, value):
        vec[index : index + 1, :width] = vec[index : index + 1, :width] + value

    def middle_rows(i, carry):
        rows = block(i, part_rows)
        after = r.rows[rows]
        result = r.acc[rows, :width] + after + bias_down
        r.x_in[i] = turned(eye, result.astype(BF16)).astype(BF16)
        normed, inverse = norm_rows(after)
        grad = r.acc[pl.ds(pl.multiple_of(seq + i * part_rows, part_rows), part_rows), :width]
        cot = r.grad[rows].astype(F32)
        add_vector(3, column_sum(grad * normed))
        add_vector(4, column_sum(grad))
        add_vector(5, column_sum(cot))
        grad_after = cot + norm_rows_back(grad * gain2, normed, inverse)
        r.rows[rows] = grad_after
        r.grad[rows] = grad_after.astype(BF16)
        return carry

    lax.fori_loop(0, PARTS, middle_rows, 0)
    r.g[:, :width] = dot(r.grad[...], r.square[0], NT).astype(BF16)
    w_query = local(4, r.w_qkv.at[0], r.square.at[0])
    w_query.start()

    def head_step(s, carry):
        def one(h, carry):
            head_back(h, head_at(h), r.q, r.k, r.v, r.g, r.bias)
            return carry

        lax.fori_loop(s * group, (s + 1) * group, one, 0)
        reducer.step(done + s)
        return carry

    lax.fori_loop(0, heads // group, head_step, 0)
    done += heads // group

    def first_again(i, carry):
        rows = block(i, part_rows)
        normed, _ = norm_rows(r.x[rows].astype(F32))
        r.h[rows] = (normed * gain1 + bias1).astype(BF16)
        return carry

    lax.fori_loop(0, PARTS, first_again, 0)
    lefts = [(r.m, r.grad), (r.q, r.h), (r.k, r.h), (r.v, r.h)]
    size = 2 * feat

    def tail_put(turn):
        pair, quarter = turn // PARTS, turn % PARTS
        return local(
            8 + turn % 2,
            r.stage.at[pl.ds(size * (turn % 2), size)],
            r.parts.at[quarter // 2, quarter % 2, pl.ds(2 * ff + size * pair, size)],
        )

    for turn in range(2 * PARTS):
        pair, quarter = turn // PARTS, turn % PARTS
        start = feat * quarter // LANES * LANES
        offset = feat * quarter - start
        products = [
            dot(one[:, start : start + 384], two[...], TN)
            for one, two in lefts[2 * pair : 2 * pair + 2]
        ]
        if turn >= 2 and turn % PARTS >= 2:
            tail_put(turn - 2).wait()
        for p in range(5):
            units = [
                products[u // 5][offset + u % 5 * HD : offset + u % 5 * HD + HD]
                for u in (2 * p, 2 * p + 1)
            ]
            at = size * (turn % 2) + 2 * HD * p
            r.stage[at : at + 2 * HD] = jnp.concatenate(units, axis=0).astype(BF16)
        tail_put(turn).start()
        if turn % PARTS == PARTS - 1:
            tail_put(turn - 1).wait()
            tail_put(turn).wait()
            reducer.step(jnp.int32(done))
            done += 1
    w_query.wait()
    r.acc[upper, :width] = dot(r.q[:, :width], r.square[0], NT)
    r.acc[upper, :width] += dot(r.k[:, :width], r.square[1], NT)
    reducer.step(jnp.int32(done))
    done += 1
    r.acc[upper, :width] += dot(r.v[:, :width], r.square[2], NT)

    def last_norm(i, carry):
        rows = block(i, part_rows)
        normed, inverse = norm_rows(r.x[rows].astype(F32))
        grad = r.acc[rows, :width]
        add_vector(1, column_sum(grad * normed))
        add_vector(2, column_sum(grad))
        back = r.rows[rows] + norm_rows_back(grad * gain1, normed, inverse)
        r.c_in[i] = turned(eye, back.astype(BF16)).astype(BF16)
        return carry

    lax.fori_loop(0, PARTS, last_norm, 0)

    steps = reducer.rounds + 11
    outs, outs_own = spread(2, r.x_in, r.output)
    grads, grads_own = spread(3, r.c_in, r.input_grad)
    turn = 32 * narrow
    lane = lax.broadcasted_iota(jnp.int32, (1, LANES), 1)

    def mix(tile, mask, value):
        lanes = pl.ds(pl.multiple_of(tile * LANES, LANES), LANES)
        r.acc[:, lanes] = jnp.where(mask, value, r.acc[:, lanes])

    def settle(j):
        base = pl.multiple_of(j * 2 * LANES, 2 * LANES)
        place = pl.multiple_of(turn + j * LANES, 32)
        get = local(4, r.total.at[pl.ds(base, 2 * LANES)], r.stage.at[pl.ds(0, 2 * LANES)])
        get.start()
        get.wait()
        give = local(5, r.stage.at[pl.ds(0, LANES)], r.down.at[pl.ds(place, LANES)])
        give.start()
        value = pltpu.roll(turned(eye, r.stage[LANES : 2 * LANES]), turn, 1)
        mix(j, lane >= turn, value)
        mix(j + 1, lane < turn, value)
        give.wait()

    def settle_left():
        get = local(4, r.total.at[pl.ds(2 * LANES * main, 2 * left)], r.stage.at[pl.ds(0, 2 * left)])
        get.start()
        get.wait()
        gives = []
        for piece in range(left // 32):
            place = lax.rem(turn + main * LANES + 32 * piece, ff)
            gives.append(
                local(
                    8 + piece,
                    r.stage.at[pl.ds(32 * piece, 32)],
                    r.down.at[pl.ds(pl.multiple_of(place, 32), 32)],
                )
            )
            gives[-1].start()
        value = turned(eye, r.stage[left : left + LANES])
        mix(main, (lane >= turn) & (lane < left), pltpu.roll(value, turn, 1))
        mix(0, lane < turn, pltpu.roll(value, lax.rem(turn + LANES - left, LANES), 1))
        r.square[0] = r.acc[:, :ff].astype(BF16)
        local(6, r.square.at[0], r.up).start()
        for copy in gives:
            copy.wait()

    def drain(t, carry):
        reducer.step(t)

        @pl.when(t == reducer.rounds + 1)
        def _():
            for copy in outs + [outs_own] + grads + [grads_own]:
                copy.start()

        vector_sum.step(t - reducer.rounds)
        at = t - done
        pl.when(at < main)(lambda: settle(at))
        pl.when(at == main)(settle_left)
        return carry

    lax.fori_loop(done, steps, drain, 0)
    finish = local(7, vec, r.vector)
    finish.start()
    for copy in outs + [outs_own] + grads + [grads_own]:
        copy.wait()
    local(6, r.square.at[0], r.up).wait()
    finish.wait()


def tokens_peer(reducer, d):
    return (reducer.at_core, reducer.at_y, reducer.at_cross)[d][1]


def softmax_parts(scores):
    expo = jnp.exp(scores - jnp.max(scores, axis=1, keepdims=True))
    return expo * (1.0 / jnp.sum(expo, axis=1, keepdims=True))


def attend_heads(pair, q_ref, k_ref, v_ref, out_ref, bias_ref):
    half = q_ref.shape[0] // 2
    results = []
    for h, start in pair:
        window = pl.ds(start, 256)
        mask = head_mask(h, start, 256)
        query = jnp.where(mask, q_ref[:, window], 0)
        keys, values = k_ref[:, window], v_ref[:, window]
        for part in range(2):
            count = (part + 1) * half
            rows = slice(part * half, count)
            scores = dot(query[rows], keys[:count], NT) * SCALE + bias_ref[rows, :count]
            probs = softmax_parts(scores).astype(BF16)
            mixed = dot(probs, values[:count], NN).astype(BF16)
            results.append((rows, window, mask, mixed))
    for rows, window, mask, mixed in results:
        out_ref[rows, window] = jnp.where(mask, mixed, out_ref[rows, window])


def head_back(h, start, q_ref, k_ref, v_ref, grad_ref, bias_ref):
    half = q_ref.shape[0] // 2
    window = pl.ds(start, 256)
    mask = head_mask(h, start, 256)
    query = jnp.where(mask, q_ref[:, window], 0)
    grad = jnp.where(mask, grad_ref[:, window], 0)
    keys, values = k_ref[:, window], v_ref[:, window]
    grads = []
    for part in range(2):
        count = (part + 1) * half
        rows = slice(part * half, count)
        scores = dot(query[rows], keys[:count], NT) * SCALE + bias_ref[rows, :count]
        grad_probs = dot(grad[rows], values[:count], NT)
        probs = softmax_parts(scores)
        inner = jnp.sum(probs * grad_probs, axis=1, keepdims=True)
        grad_scores = (probs * (grad_probs - inner) * SCALE).astype(BF16)
        gq = dot(grad_scores, keys[:count], NN).astype(BF16)
        gk = dot(grad_scores, query[rows], TN)
        gv = dot(probs.astype(BF16), grad[rows], TN)
        grads.append((gq, gk, gv))
    (gq0, gk0, gv0), (gq1, gk1, gv1) = grads
    q_ref[:half, window] = jnp.where(mask, gq0, q_ref[:half, window])
    q_ref[half:, window] = jnp.where(mask, gq1, q_ref[half:, window])
    for ref, first, second in ((k_ref, gk0, gk1), (v_ref, gv0, gv1)):
        top, bottom = (first + second[:half]).astype(BF16), second[half:].astype(BF16)
        ref[:half, window] = jnp.where(mask, top, ref[:half, window])
        ref[half:, window] = jnp.where(mask, bottom, ref[half:, window])


def whole_layer(**arrays):
    parts, width, part_rows = arrays["tokens"].shape
    seq, hidden = parts * part_rows, arrays["w_up"].shape[1]
    ff = hidden // parts
    rows = 2 * ff + width
    reducer = Reducer(128, 96, width)
    scratch = reducer.scratch()
    low = lambda *shape: pltpu.VMEM(shape, BF16)
    full = lambda *shape: pltpu.VMEM(shape, F32)
    dma = lambda *shape: pltpu.SemaphoreType.DMA(shape)
    scratch.update(
        x_in=low(parts, width, part_rows),
        c_in=low(parts, width, part_rows),
        w_up_in=low(2, width, parts * LANES),
        w_down_in=low(2, width, parts * LANES),
        stage=low(width, width),
        square=low(3, width, width),
        q=low(seq, WIDE),
        k=low(seq, WIDE),
        v=low(seq, WIDE),
        m=low(seq, WIDE),
        g=low(seq, WIDE),
        h=low(seq, width),
        grad=low(seq, width),
        x=low(seq, width),
        rows=full(seq, width),
        acc=full(width, WIDE),
        bias=full(seq, seq),
        up_bias=full(1, hidden),
        vec=full(8, hidden),
        vec_in=full(6, 8, hidden),
        vec_send=dma(6),
        vec_recv=dma(6),
        local=dma(12),
        w_load=dma(2, 2, parts),
        spread_send=dma(4, 3),
        spread_recv=dma(4, 3),
    )
    hbm = pl.BlockSpec(memory_space=pl.ANY)
    vmem = pl.BlockSpec(memory_space=pltpu.VMEM)
    low_out = lambda *shape: jax.ShapeDtypeStruct(shape, BF16)
    outputs = dict(
        parts=low_out(2, parts // 2, rows, width),
        total=low_out(rows, width),
        down=low_out(ff, width),
        up=low_out(width, ff),
        output=low_out(parts, width, part_rows),
        input_grad=low_out(parts, width, part_rows),
        vector=jax.ShapeDtypeStruct((8, hidden), F32),
    )
    smem = pl.BlockSpec(memory_space=pltpu.SMEM)
    names = list(arrays) + list(outputs) + list(scratch)
    results = pl.pallas_call(
        functools.partial(layer_kernel, reducer, names),
        out_shape=tuple(outputs.values()),
        in_specs=[hbm] * 6 + [smem] + [vmem] * (len(arrays) - 7),
        out_specs=[hbm] * len(outputs),
        scratch_shapes=list(scratch.values()),
        compiler_params=pltpu.CompilerParams(
            collective_id=0, has_side_effects=True, vmem_limit_bytes=VMEM_LIMIT
        ),
        name="whole_layer",
    )(*arrays.values())
    return types.SimpleNamespace(**dict(zip(outputs, results)))


def on_device(
    wide,
    tokens,
    lengths,
    norm1_gain,
    norm1_bias,
    w_qkv,
    w_out,
    norm2_gain,
    norm2_bias,
    w_up,
    bias_up,
    w_down,
    bias_down,
    cotangent,
):
    narrow = lax.axis_index("narrow")
    width, hidden = w_up.shape
    parts = tokens.shape[0]
    ff, feat = hidden // parts, width // parts
    got = whole_layer(
        tokens=tokens.transpose(0, 2, 1),
        cot=cotangent.transpose(0, 2, 1),
        w_qkv=w_qkv.transpose(1, 0, 2),
        w_out=w_out,
        w_up=w_up,
        w_down=w_down.T,
        lengths=lengths,
        gain1=norm1_gain,
        bias1=norm1_bias,
        gain2=norm2_gain,
        bias2=norm2_bias,
        bias_up=bias_up,
        bias_down=bias_down,
    )
    rest, down, up, vector = got.total[2 * ff :], got.down, got.up, got.vector
    if wide > BLOCK:
        groups = [list(range(i, wide, BLOCK)) for i in range(BLOCK)]
        rest, down, up, vector = (
            lax.psum(a.astype(F32), "wide", axis_index_groups=groups)
            for a in (rest, down, up, vector)
        )
    qkv = rest[feat:].astype(F32).reshape(3, feat, width).transpose(2, 0, 1)
    mine = lambda v: lax.dynamic_slice_in_dim(v, narrow * (v.shape[0] // parts), v.shape[0] // parts)
    up_bias = mine(vector[0])
    gain1, bias1, gain2, bias2, down_bias = (mine(vector[i, :width]) for i in range(1, 6))
    return (
        got.output.transpose(0, 2, 1),
        got.input_grad.transpose(0, 2, 1).astype(F32),
        gain1,
        bias1,
        qkv,
        rest[:feat].astype(F32),
        gain2,
        bias2,
        up.astype(F32),
        up_bias,
        down.astype(F32),
        down_bias,
    )


def solution(mesh):
    rows = P("wide", "narrow", None)
    in_specs = (rows, P("wide")) + (P(),) * 10 + (rows,)
    out_specs = (
        rows,
        rows,
        P("narrow"),
        P("narrow"),
        P(None, None, "narrow"),
        P("narrow", None),
        P("narrow"),
        P("narrow"),
        P(None, "narrow"),
        P("narrow"),
        P("narrow", None),
        P("narrow"),
    )
    return jax.shard_map(
        functools.partial(on_device, mesh.shape["wide"]),
        mesh=mesh,
        in_specs=in_specs,
        out_specs=out_specs,
        check_vma=False,
    )
```

time: 977 us -> 287 us (0.29)
  waiting for transfers between devices: 426 us -> 0 us
  Pallas kernels: 0 us -> 261 us
  matrix products: 213 us -> 0 us
  blocking collectives: 131 us -> 0 us
  local copies, waits for them, and re-layouts: 126 us -> 7.35 us
  starting transfers between devices: 23.7 us -> 0 us
  other arithmetic: 32 us -> 12.5 us
  between operations: 15.2 us -> 0.88 us
    psum x1 -> x0, waiting for transfers between devices: 264 us -> none  [on_device(): lax.psum((gain_one, bias_one, qkv_total, out_share, gain_two, bias_two, u...]
    pallas_call x0 -> x1, Pallas kernels: none -> 261 us  [whole_layer(): pl.pallas_call(functools.partial(layer_kernel, reducer, names), out_shape...]
    dot_general x40 -> x0, matrix products: 213 us -> none  [the longest x4 34.9 us: cell_attention_back(): jnp.einsum('hqk,khe->qhe', grad_scores, keys, preferred_element_type=jnp....]
    all_to_all x5 -> x0, waiting for transfers between devices: 161 us -> none  [the longest x1 63.2 us: on_device(): lax.all_to_all(projected, 'narrow', split_axis=3, concat_axis=1, tiled=True)]
    psum x1 -> x0, blocking collectives: 95.5 us -> none  [on_device(): lax.psum((gain_one, bias_one, qkv_total, out_share, gain_two, bias_two, u...]
    all_to_all x8 -> x0, local copies, waits for them, and re-layouts: 37.6 us -> none  [the longest x2 12.5 us: on_device(): lax.all_to_all(projected, 'narrow', split_axis=3, concat_axis=1, tiled=True)]
    convert_element_type x4 -> x0, local copies, waits for them, and re-layouts: 32.2 us -> none  [the longest x1 9.65 us: on_device(): projected = jnp.einsum('cpd,dke->cpke', hidden1, w_qkv, preferred_element...]
    all_to_all x1 -> x0, blocking collectives: 24.5 us -> none  [on_device(): lax.all_to_all(attended, 'narrow', split_axis=1, concat_axis=2, tiled=True)]
  transfers between devices with their start and end apart: 10 -> 0, of which waited for: 5 -> 0; matrix products, arithmetic and copies ran while one was open for 35% -> 0% of each run, Pallas kernels for 0% -> 0%
where the time goes in v1:
time: 287 us; the launch traced here: 282 us
  Pallas kernels  261 us (91%)
  other arithmetic  12.5 us (4%)
  local copies, waits for them, and re-layouts  7.35 us (3%)
    pallas_call x1, Pallas kernels, whole_layer(): pl.pallas_call(functools.partial(layer_kernel, reducer, names), out_shape...  261 us

profile of v1, /device:TPU:0, one launch (start us, length us, event | category | flops | bytes accessed | tf_op | source)
XLA Modules:
  0.0 281.7 jit_solution(2147094456904975904)
XLA Ops:
  0.6 261.0 %whole_layer.1 = (bf16[2,2,3360,1120]{3,2,1,0:T(8,128)(2,1)}, bf16[3360,1120]{1,0:T(8,128)(2,1)}, bf16[1120,1120]{1,0:T(8,128)(2,1)}, bf16[1120,1120]{1,0:T(8,12...) custom-call(bf16[4,1120,128]{2,1,0:T(8,128)(2,1)} %bitcast.15, ...), custom_call_target="tpu_custom_call" | custom-call | tf_op jit(solution)/shard_map/whole_layer/pallas_call | solution.py:1012
  261.6 2.8 convert_bitcast_fusion.1
  264.4 1.0 fusion
  265.5 0.7 dynamic-slice_reduce_fusion.5
  266.1 0.7 dynamic-slice_reduce_fusion.3
  266.8 1.7 slice.29
  268.5 0.0 copy-start.1
  268.5 2.2 convert_bitcast_fusion
  270.7 2.2 slice_convert_fusion
  272.9 0.7 dynamic-slice_reduce_fusion.1
  273.5 0.0 copy-done.1
  273.5 0.0 copy-start
  273.5 2.7 convert_element_type.19
  276.2 0.9 slice.33
  277.1 0.7 dynamic-slice_reduce_fusion
  277.8 0.0 copy-done
  277.8 0.0 copy-start.2
  277.8 2.7 convert_element_type.20
  280.5 0.0 copy-done.2
  280.5 1.0 copy.26
Async XLA Ops:
  268.5 5.1 %copy-start.1 = (bf16[1120,1120]{1,0:T(8,128)(2,1)S(1)}, bf16[1120,1120]{1,0:T(8,128)(2,1)}, u32[]{:S(2)}) copy-start(bf16[1120,1120]{1,0:T(8,128)(2,1)} %get-tuple-element.22) | copy-start | bytes 7526404
  273.5 4.3 %copy-start = (bf16[1120,1120]{1,0:T(8,128)(2,1)S(1)}, bf16[1120,1120]{1,0:T(8,128)(2,1)}, u32[]{:S(2)}) copy-start(bf16[1120,1120]{1,0:T(8,128)(2,1)} %get-tuple-element.23) | copy-start | bytes 7526404
  277.8 2.7 copy-start.2

commit v2 on v1

--- a/solution.py
+++ b/solution.py
@@ -15,7 +15,7 @@
 VMEM_LIMIT = 62 * 1024 * 1024
 LINE, PAIR = 4, 2
 BLOCK = LINE * PAIR
-SLOTS, STATES, STATES_A = 4, 11, 8
+SLOTS = 4
 CORE, CY, CA, CB, CC, CX, AX, AY, A1, A2, A3, AG, GATHER = range(13)
 CHANNELS = GATHER + 6
 
@@ -35,7 +35,9 @@
 class Reducer:
     hops = 9
 
-    def __init__(self, rows_c, rows_a, width):
+    def __init__(self, rows_c, rows_a, width, total):
+        self.rounds = total // (rows_c + rows_a)
+        self.states, self.states_a = 10, 8
         self.rows_c, self.rows_a, self.width = rows_c, rows_a, width
         self.rows = rows_c + rows_a
         self.shard, self.half = rows_c // LINE, rows_a // 2
@@ -44,10 +46,10 @@
         c, a, q, h, d = self.rows_c, self.rows_a, self.shard, self.half, self.width
         buffers = dict(
             own=(2, self.rows, d),
-            core_in=(SLOTS, 2, self.rows, d),
+            core_in=(2, 2, self.rows, d),
             cy_out=(2, c, d),
             cy_in=(SLOTS, c, d),
-            c_state=(STATES, c, d),
+            c_state=(self.states, c, d),
             ca_in=(SLOTS, 3 * q, d),
             cb_in=(SLOTS, 2 * q, d),
             cc_in=(SLOTS, q, d),
@@ -60,7 +62,7 @@
             a_sum=(4, h, d),
             a1_in=(SLOTS, h, d),
             a2_in=(SLOTS, h, d),
-            a_state=(STATES_A, 2, h, d),
+            a_state=(self.states_a, 2, h, d),
         )
         result = {name: pltpu.VMEM(shape, BF16) for name, shape in buffers.items()}
         result.update(
@@ -85,7 +87,6 @@
         self.at_x = (flip(wide, self.x), narrow)
         self.at_up = (wide + PAIR, narrow)
         self.at_down = (wide - PAIR, narrow)
-        self.rounds = out_ref.shape[0] // self.rows
 
     def barrier(self):
         z = self.z
@@ -127,7 +128,7 @@
             CORE,
             k,
             self.part_ref.at[:, 1 - self.core, pl.ds(k * self.rows, self.rows)],
-            self.refs.core_in.at[lax.rem(k, SLOTS)],
+            self.refs.core_in.at[lax.rem(k, 2)],
             self.at_core,
         )
 
@@ -139,7 +140,7 @@
 
     def c_rows(self, k, first, count):
         return self.refs.c_state.at[
-            lax.rem(k, STATES), pl.ds(pl.multiple_of(first * self.shard, self.shard), count * self.shard)
+            lax.rem(k, self.states), pl.ds(pl.multiple_of(first * self.shard, self.shard), count * self.shard)
         ]
 
     def line_hops(self, k):
@@ -180,7 +181,7 @@
     def sum_hops(self, k):
         z, slot = self.z, lax.rem(k, 4)
         own = self.refs.a_sum.at[slot]
-        final = self.refs.a_state.at[lax.rem(k, STATES_A), self.x]
+        final = self.refs.a_state.at[lax.rem(k, self.states_a), self.x]
         return {
             A1: [
                 (z == 0, self.slotted(A1, k, own, self.at_up)),
@@ -197,14 +198,14 @@
         }
 
     def store(self, k):
-        r, slot, two = self.refs, lax.rem(k, STATES), lax.rem(k, 2)
+        r, slot, two = self.refs, lax.rem(k, self.states), lax.rem(k, 2)
         base = k * self.rows
         yield pltpu.make_async_copy(
             r.c_state.at[slot], self.out_ref.at[pl.ds(base, self.rows_c)], r.c_store.at[two]
         )
 
     def store_a(self, k):
-        r, slot, two = self.refs, lax.rem(k, STATES_A), lax.rem(k, 2)
+        r, slot, two = self.refs, lax.rem(k, self.states_a), lax.rem(k, 2)
         base = k * self.rows + self.rows_c
         for i in range(2):
             yield pltpu.make_async_copy(
@@ -233,14 +234,13 @@
             self.core_hop(k).start()
             pl.when(k == 0)(self.load(k).start)
 
-        stage(0, begin)
 
         def after_core(k):
             two, four = lax.rem(k, 2), lax.rem(k, SLOTS)
             copy = self.core_hop(k)
             copy.wait()
             self.load(k).wait()
-            total = lambda i, rows: r.own[i, rows] + r.core_in[four, i, rows]
+            total = lambda i, rows: r.own[i, rows] + r.core_in[two, i, rows]
             everything = pl.ds(0, c)
             r.cy_out[two] = total(1 - y, everything)
             self.cy_hop(k).start()
@@ -248,16 +248,17 @@
                 rows = pl.ds(pl.multiple_of(c + (1 - x) * h, 16), h)
                 r.ax_out[two, i] = total(i, rows)
             self.ax_hop(k).start()
-            r.c_state[lax.rem(k, STATES), :] = total(y, everything)
+            r.c_state[lax.rem(k, self.states), :] = total(y, everything)
             for i in range(2):
                 rows = pl.ds(pl.multiple_of(c + x * h, 16), h)
                 r.ax_keep[two, i] = total(i, rows)
             pl.when(k + 1 < self.rounds)(lambda: self.load(k + 1).start())
 
         stage(1, after_core)
+        stage(0, begin)
 
         def second(k):
-            two, four, slot = lax.rem(k, 2), lax.rem(k, SLOTS), lax.rem(k, STATES)
+            two, four, slot = lax.rem(k, 2), lax.rem(k, SLOTS), lax.rem(k, self.states)
             self.cy_hop(k).wait()
             r.c_state[slot] = r.c_state[slot] + r.cy_in[four]
             start_if(self.line_hops(k)[0][1])
@@ -318,7 +319,7 @@
             @pl.when((z > 0) & (z < LINE - 1))
             def _():
                 hops[A2][0][1].wait_recv()
-                r.a_state[lax.rem(k, STATES_A), x] = r.a_sum[slot] + r.a2_in[four]
+                r.a_state[lax.rem(k, self.states_a), x] = r.a_sum[slot] + r.a2_in[four]
 
             start_if(hops[A3])
 
@@ -387,7 +388,7 @@
         return self.slotted(CX, k, self.c_rows(k, self.z, 1), self.at_x)
 
     def ag_hop(self, k):
-        final = self.refs.a_state.at[lax.rem(k, STATES_A), self.x]
+        final = self.refs.a_state.at[lax.rem(k, self.states_a), self.x]
         return self.copy(AG, k, final, final, self.at_x)
 
 
@@ -525,7 +526,7 @@
     main = ff // LANES
     left = ff - main * LANES
     stride = (r.w_up.shape[1] // LANES - main) // (PARTS - 1)
-    heads, group = width // HD, 5
+    heads, group = width // HD, 4
     reducer.bind(r.parts, r.total, r)
     narrow, y = reducer.narrow, reducer.y
     gain1, bias1, gain2, bias2, bias_down = (
@@ -533,6 +534,7 @@
     )
     eye = identity(LANES)
     vec = r.vec
+    stage = r.square.at[2]
     vector_sum = VectorSum(reducer, vec, r.vec_in, r.vec_send, r.vec_recv)
 
     def local(index, source, target):
@@ -575,6 +577,8 @@
     cots, cots_own = spread(1, r.cot, r.c_in)
     for copy in tokens + [tokens_own]:
         copy.start()
+    cots[0].start()
+    cots_own.start()
     for copy in weights(0, main_tiles(0)):
         copy.start()
     vec[...] = jnp.zeros_like(vec)
@@ -584,7 +588,7 @@
     row = lax.broadcasted_iota(jnp.int32, (seq, seq), 0)
     column = lax.broadcasted_iota(jnp.int32, (seq, seq), 1)
     length = r.lengths[narrow]
-    r.bias[...] = jnp.where((column <= row) & (column < length), 0.0, -1e30)
+    r.bias[...] = jnp.where((column <= row) & (column < length), 0.0, -1e30).astype(BF16)
     r.up_bias[...] = r.bias_up[...].reshape(r.up_bias.shape)
 
     def first_norm(i):
@@ -607,10 +611,11 @@
         copy.wait()
     project(y)
     for d in (1, 2):
-        tokens[d].wait()
+        tokens[d].wait_send()
+        cots[d].start()
+    for d in (1, 2):
+        tokens[d].wait_recv()
         first_norm(tokens_peer(reducer, d))
-    for copy in cots + [cots_own]:
-        copy.start()
     project(1 - y)
     w_out = local(4, r.w_out, r.square.at[0])
     w_out.start()
@@ -647,7 +652,7 @@
         return [
             local(
                 8 + q,
-                r.stage.at[pl.ds(2 * LANES * q, count)],
+                stage.at[pl.ds(2 * LANES * q, count)],
                 r.parts.at[q // 2, q % 2, pl.ds(base, count)],
             )
             for q in range(PARTS)
@@ -695,7 +700,7 @@
 
         for j, value in enumerate(values):
             for q in range(PARTS):
-                r.stage[LANES * (2 * q + j) : LANES * (2 * q + j + 1)] = value[
+                stage[LANES * (2 * q + j) : LANES * (2 * q + j + 1)] = value[
                     LANES * q : LANES * (q + 1)
                 ]
         for copy in put_block(i):
@@ -725,7 +730,7 @@
         for q, pieces in enumerate(leftover_rows(tiles)):
             at = 2 * LANES * q + left * j
             for piece in pieces:
-                r.stage[at : at + piece.shape[0]] = piece
+                stage[at : at + piece.shape[0]] = piece
                 at += piece.shape[0]
     put_left = put(2 * left, 2 * LANES * main)
     for copy in put_left:
@@ -755,9 +760,37 @@
         return carry
 
     lax.fori_loop(0, PARTS, middle_rows, 0)
+    four = 4 * HD
+    early = []
+    for quarter in range(PARTS):
+        start = feat * quarter // LANES * LANES
+        offset = feat * quarter - start
+        product = dot(r.m[:, start : start + 384], r.grad[...], TN)
+        for p in range(2):
+            at = four * quarter + 2 * HD * p
+            first = offset + 2 * HD * p
+            stage[at : at + 2 * HD] = product[first : first + 2 * HD].astype(BF16)
+        r.acc[HD * quarter : HD * (quarter + 1), :width] = product[
+            offset + four : offset + four + HD
+        ]
+        early.append(
+            local(
+                8 + quarter,
+                stage.at[pl.ds(four * quarter, four)],
+                r.parts.at[quarter // 2, quarter % 2, pl.ds(2 * ff, four)],
+            )
+        )
+        early[-1].start()
     r.g[:, :width] = dot(r.grad[...], r.square[0], NT).astype(BF16)
+    for copy in early:
+        copy.wait()
     w_query = local(4, r.w_qkv.at[0], r.square.at[0])
     w_query.start()
+    reducer.step(jnp.int32(done))
+    done += 1
+    outs, outs_own = spread(2, r.x_in, r.output)
+    for copy in outs + [outs_own]:
+        copy.start()
 
     def head_step(s, carry):
         def one(h, carry):
@@ -778,45 +811,46 @@
         return carry
 
     lax.fori_loop(0, PARTS, first_again, 0)
-    lefts = [(r.m, r.grad), (r.q, r.h), (r.k, r.h), (r.v, r.h)]
-    size = 2 * feat
+    sizes = (width - 2 * feat - four, 2 * feat)
+    bases = (2 * ff + four, 2 * ff + width - 2 * feat)
 
     def tail_put(turn):
         pair, quarter = turn // PARTS, turn % PARTS
         return local(
             8 + turn % 2,
-            r.stage.at[pl.ds(size * (turn % 2), size)],
-            r.parts.at[quarter // 2, quarter % 2, pl.ds(2 * ff + size * pair, size)],
+            stage.at[pl.ds(2 * feat * (turn % 2), sizes[pair])],
+            r.parts.at[quarter // 2, quarter % 2, pl.ds(bases[pair], sizes[pair])],
         )
 
     for turn in range(2 * PARTS):
         pair, quarter = turn // PARTS, turn % PARTS
         start = feat * quarter // LANES * LANES
         offset = feat * quarter - start
-        products = [
-            dot(one[:, start : start + 384], two[...], TN)
-            for one, two in lefts[2 * pair : 2 * pair + 2]
-        ]
+        units = [] if pair else [r.acc[HD * quarter : HD * (quarter + 1), :width]]
+        for left_ref, right_ref in ((r.k, r.h), (r.v, r.h)) if pair else ((r.q, r.h),):
+            product = dot(left_ref[:, start : start + 384], right_ref[...], TN)
+            units += [product[offset + HD * u : offset + HD * (u + 1)] for u in range(5)]
         if turn >= 2 and turn % PARTS >= 2:
             tail_put(turn - 2).wait()
-        for p in range(5):
-            units = [
-                products[u // 5][offset + u % 5 * HD : offset + u % 5 * HD + HD]
-                for u in (2 * p, 2 * p + 1)
-            ]
-            at = size * (turn % 2) + 2 * HD * p
-            r.stage[at : at + 2 * HD] = jnp.concatenate(units, axis=0).astype(BF16)
+        for p in range(len(units) // 2):
+            at = 2 * feat * (turn % 2) + 2 * HD * p
+            stage[at : at + 2 * HD] = jnp.concatenate(units[2 * p : 2 * p + 2], axis=0).astype(
+                BF16
+            )
         tail_put(turn).start()
         if turn % PARTS == PARTS - 1:
             tail_put(turn - 1).wait()
             tail_put(turn).wait()
             reducer.step(jnp.int32(done))
             done += 1
+    w_value = local(3, r.w_qkv.at[2], r.square.at[2])
+    w_value.start()
     w_query.wait()
     r.acc[upper, :width] = dot(r.q[:, :width], r.square[0], NT)
     r.acc[upper, :width] += dot(r.k[:, :width], r.square[1], NT)
     reducer.step(jnp.int32(done))
     done += 1
+    w_value.wait()
     r.acc[upper, :width] += dot(r.v[:, :width], r.square[2], NT)
 
     def last_norm(i, carry):
@@ -832,7 +866,6 @@
     lax.fori_loop(0, PARTS, last_norm, 0)
 
     steps = reducer.rounds + 11
-    outs, outs_own = spread(2, r.x_in, r.output)
     grads, grads_own = spread(3, r.c_in, r.input_grad)
     turn = 32 * narrow
     lane = lax.broadcasted_iota(jnp.int32, (1, LANES), 1)
@@ -844,18 +877,18 @@
     def settle(j):
         base = pl.multiple_of(j * 2 * LANES, 2 * LANES)
         place = pl.multiple_of(turn + j * LANES, 32)
-        get = local(4, r.total.at[pl.ds(base, 2 * LANES)], r.stage.at[pl.ds(0, 2 * LANES)])
+        get = local(4, r.total.at[pl.ds(base, 2 * LANES)], stage.at[pl.ds(0, 2 * LANES)])
         get.start()
         get.wait()
-        give = local(5, r.stage.at[pl.ds(0, LANES)], r.down.at[pl.ds(place, LANES)])
+        give = local(5, stage.at[pl.ds(0, LANES)], r.down.at[pl.ds(place, LANES)])
         give.start()
-        value = pltpu.roll(turned(eye, r.stage[LANES : 2 * LANES]), turn, 1)
+        value = pltpu.roll(turned(eye, stage[LANES : 2 * LANES]), turn, 1)
         mix(j, lane >= turn, value)
         mix(j + 1, lane < turn, value)
         give.wait()
 
     def settle_left():
-        get = local(4, r.total.at[pl.ds(2 * LANES * main, 2 * left)], r.stage.at[pl.ds(0, 2 * left)])
+        get = local(4, r.total.at[pl.ds(2 * LANES * main, 2 * left)], stage.at[pl.ds(0, 2 * left)])
         get.start()
         get.wait()
         gives = []
@@ -864,12 +897,12 @@
             gives.append(
                 local(
                     8 + piece,
-                    r.stage.at[pl.ds(32 * piece, 32)],
+                    stage.at[pl.ds(32 * piece, 32)],
                     r.down.at[pl.ds(pl.multiple_of(place, 32), 32)],
                 )
             )
             gives[-1].start()
-        value = turned(eye, r.stage[left : left + LANES])
+        value = turned(eye, stage[left : left + LANES])
         mix(main, (lane >= turn) & (lane < left), pltpu.roll(value, turn, 1))
         mix(0, lane < turn, pltpu.roll(value, lax.rem(turn + LANES - left, LANES), 1))
         r.square[0] = r.acc[:, :ff].astype(BF16)
@@ -880,19 +913,27 @@
     def drain(t, carry):
         reducer.step(t)
 
-        @pl.when(t == reducer.rounds + 1)
+        @pl.when(t == done + 3)
         def _():
-            for copy in outs + [outs_own] + grads + [grads_own]:
+            for copy in grads + [grads_own]:
                 copy.start()
 
-        vector_sum.step(t - reducer.rounds)
+        vector_sum.step(t - done)
         at = t - done
-        pl.when(at < main)(lambda: settle(at))
-        pl.when(at == main)(settle_left)
+        for i in range(2):
+            pl.when(at < 3)(functools.partial(settle, 2 * at + i))
+        pl.when(at == 3)(lambda: settle(6))
+        pl.when(at == 5)(lambda: settle(7))
+        pl.when(at == 6)(settle_left)
         return carry
 
     lax.fori_loop(done, steps, drain, 0)
-    finish = local(7, vec, r.vector)
+    first = vec[0:1]
+    others = vec[:, :WIDE]
+    r.share[...] = pltpu.roll(others, lax.rem(WIDE - feat * narrow, WIDE), 1)
+    hidden = PARTS * ff
+    r.share[0:1, :ff] = pltpu.roll(first, lax.rem(hidden - ff * narrow, hidden), 1)[:, :ff]
+    finish = local(7, r.share, r.vector)
     finish.start()
     for copy in outs + [outs_own] + grads + [grads_own]:
         copy.wait()
@@ -962,7 +1003,7 @@
     seq, hidden = parts * part_rows, arrays["w_up"].shape[1]
     ff = hidden // parts
     rows = 2 * ff + width
-    reducer = Reducer(128, 96, width)
+    reducer = Reducer(128, 96, width, rows)
     scratch = reducer.scratch()
     low = lambda *shape: pltpu.VMEM(shape, BF16)
     full = lambda *shape: pltpu.VMEM(shape, F32)
@@ -972,7 +1013,6 @@
         c_in=low(parts, width, part_rows),
         w_up_in=low(2, width, parts * LANES),
         w_down_in=low(2, width, parts * LANES),
-        stage=low(width, width),
         square=low(3, width, width),
         q=low(seq, WIDE),
         k=low(seq, WIDE),
@@ -984,10 +1024,11 @@
         x=low(seq, width),
         rows=full(seq, width),
         acc=full(width, WIDE),
-        bias=full(seq, seq),
+        bias=low(seq, seq),
         up_bias=full(1, hidden),
         vec=full(8, hidden),
         vec_in=full(6, 8, hidden),
+        share=full(8, WIDE),
         vec_send=dma(6),
         vec_recv=dma(6),
         local=dma(12),
@@ -1005,7 +1046,7 @@
         up=low_out(width, ff),
         output=low_out(parts, width, part_rows),
         input_grad=low_out(parts, width, part_rows),
-        vector=jax.ShapeDtypeStruct((8, hidden), F32),
+        vector=jax.ShapeDtypeStruct((8, WIDE), F32),
     )
     smem = pl.BlockSpec(memory_space=pltpu.SMEM)
     names = list(arrays) + list(outputs) + list(scratch)
@@ -1019,6 +1060,107 @@
             collective_id=0, has_side_effects=True, vmem_limit_bytes=VMEM_LIMIT
         ),
         name="whole_layer",
+    )(*arrays.values())
+    return types.SimpleNamespace(**dict(zip(outputs, results)))
+
+
+def finish_kernel(names, *refs):
+    r = types.SimpleNamespace(**dict(zip(names, refs)))
+    rows, step = r.down.shape[0], 112
+    feat = r.out.shape[0]
+
+    def copy(index, source, target):
+        return pltpu.make_async_copy(source, target, r.moves.at[index])
+
+    loads = [
+        copy(0, r.down, r.down_in),
+        copy(1, r.up, r.up_in),
+        copy(2, r.total.at[pl.ds(r.total.shape[0] - rows, rows)], r.rest_in),
+        copy(3, r.grad, r.grad_in),
+    ]
+    plain = copy(4, r.output, r.output_in)
+    for move in loads + [plain]:
+        move.start()
+    stores = []
+
+    def store(source, target):
+        stores.append(copy(5 + len(stores), source, target))
+        stores[-1].start()
+
+    r.up_bias_to[...] = r.vector[0, :rows]
+    for index, target in enumerate((r.gain1, r.bias1, r.gain2, r.bias2, r.down_bias)):
+        target[...] = r.vector[index + 1, :feat]
+    wides = ((r.down_in, r.down_wide, r.down_to), (r.up_in, r.up_wide, r.up_to))
+    for load, (source, wide, target) in zip(loads, wides):
+        load.wait()
+        for at in range(0, rows, step):
+            wide[at : at + step] = source[at : at + step].astype(F32)
+            if (at // step) % 2:
+                area = pl.ds(at - step, 2 * step)
+                store(wide.at[area], target.at[area])
+    loads[2].wait()
+    sent = 0
+    for at in range(0, rows, step):
+        r.rest_wide[at : at + step] = r.rest_in[at : at + step].astype(F32)
+        while sent < rows and at + step >= sent + feat:
+            area = pl.ds(sent, feat)
+            target = r.out if sent == 0 else r.qkv.at[pl.ds(sent - feat, feat)]
+            store(r.rest_wide.at[area], target)
+            sent += feat
+    loads[3].wait()
+    for i in range(r.grad_in.shape[0]):
+        r.grad_wide[i] = r.grad_in[i].astype(F32)
+        store(r.grad_wide.at[i], r.grad_to.at[i])
+    plain.wait()
+    store(r.output_in, r.result)
+    for move in stores:
+        move.wait()
+
+
+def finish(**arrays):
+    shape = {name: array.shape for name, array in arrays.items()}
+    rows, width = shape["down"]
+    feat = width // PARTS
+    wide = lambda *size: jax.ShapeDtypeStruct(size, F32)
+    outputs = dict(
+        result=jax.ShapeDtypeStruct(shape["output"], BF16),
+        grad_to=wide(*shape["grad"]),
+        qkv=wide(3 * feat, width),
+        out=wide(feat, width),
+        up_to=wide(*shape["up"]),
+        down_to=wide(rows, width),
+        gain1=wide(feat),
+        bias1=wide(feat),
+        gain2=wide(feat),
+        bias2=wide(feat),
+        up_bias_to=wide(rows),
+        down_bias=wide(feat),
+    )
+    kept = lambda name: pltpu.VMEM(shape[name], arrays[name].dtype)
+    square = lambda dtype: pltpu.VMEM((rows, width), dtype)
+    scratch = dict(
+        down_in=kept("down"),
+        up_in=kept("up"),
+        rest_in=square(arrays["total"].dtype),
+        grad_in=kept("grad"),
+        output_in=kept("output"),
+        down_wide=square(F32),
+        up_wide=square(F32),
+        rest_wide=square(F32),
+        grad_wide=pltpu.VMEM(shape["grad"], F32),
+        moves=pltpu.SemaphoreType.DMA((32,)),
+    )
+    hbm = pl.BlockSpec(memory_space=pl.ANY)
+    vmem = pl.BlockSpec(memory_space=pltpu.VMEM)
+    names = list(arrays) + list(outputs) + list(scratch)
+    results = pl.pallas_call(
+        functools.partial(finish_kernel, names),
+        out_shape=tuple(outputs.values()),
+        in_specs=[hbm] * (len(arrays) - 1) + [vmem],
+        out_specs=[hbm] * 6 + [vmem] * 6,
+        scratch_shapes=list(scratch.values()),
+        compiler_params=pltpu.CompilerParams(vmem_limit_bytes=VMEM_LIMIT),
+        name="finish",
     )(*arrays.values())
     return types.SimpleNamespace(**dict(zip(outputs, results)))
 
@@ -1039,10 +1181,8 @@
     bias_down,
     cotangent,
 ):
-    narrow = lax.axis_index("narrow")
-    width, hidden = w_up.shape
-    parts = tokens.shape[0]
-    ff, feat = hidden // parts, width // parts
+    width = w_out.shape[0]
+    feat = width // tokens.shape[0]
     got = whole_layer(
         tokens=tokens.transpose(0, 2, 1),
         cot=cotangent.transpose(0, 2, 1),
@@ -1058,30 +1198,33 @@
         bias_up=bias_up,
         bias_down=bias_down,
     )
-    rest, down, up, vector = got.total[2 * ff :], got.down, got.up, got.vector
     if wide > BLOCK:
         groups = [list(range(i, wide, BLOCK)) for i in range(BLOCK)]
-        rest, down, up, vector = (
+        got.total, got.down, got.up, got.vector = (
             lax.psum(a.astype(F32), "wide", axis_index_groups=groups)
-            for a in (rest, down, up, vector)
+            for a in (got.total, got.down, got.up, got.vector)
         )
-    qkv = rest[feat:].astype(F32).reshape(3, feat, width).transpose(2, 0, 1)
-    mine = lambda v: lax.dynamic_slice_in_dim(v, narrow * (v.shape[0] // parts), v.shape[0] // parts)
-    up_bias = mine(vector[0])
-    gain1, bias1, gain2, bias2, down_bias = (mine(vector[i, :width]) for i in range(1, 6))
+    last = finish(
+        output=got.output,
+        grad=got.input_grad,
+        total=got.total,
+        down=got.down,
+        up=got.up,
+        vector=got.vector,
+    )
     return (
-        got.output.transpose(0, 2, 1),
-        got.input_grad.transpose(0, 2, 1).astype(F32),
-        gain1,
-        bias1,
-        qkv,
-        rest[:feat].astype(F32),
-        gain2,
-        bias2,
-        up.astype(F32),
-        up_bias,
-        down.astype(F32),
-        down_bias,
+        last.result.transpose(0, 2, 1),
+        last.grad_to.transpose(0, 2, 1),
+        last.gain1,
+        last.bias1,
+        last.qkv.reshape(3, feat, width).transpose(2, 0, 1),
+        last.out,
+        last.gain2,
+        last.bias2,
+        last.up_to,
+        last.up_bias_to,
+        last.down_to,
+        last.down_bias,
     )
 
 

time: 287 us -> 274 us (0.955)
  other arithmetic: 12.5 us -> 0 us
  local copies, waits for them, and re-layouts: 7.35 us -> 0 us
  Pallas kernels: 261 us -> 267 us
    pallas_call x0 -> x1, Pallas kernels: none -> 10.7 us  [finish(): pl.pallas_call(functools.partial(finish_kernel, names), out_shape=tuple(o...]
    convert_element_type x4 -> x0, other arithmetic: 10.3 us -> none  [the longest x1 2.79 us: on_device(): got.input_grad.transpose(0, 2, 1).astype(F32)]
    pallas_call x1, Pallas kernels: 261 us -> 257 us  [whole_layer(): pl.pallas_call(functools.partial(layer_kernel, reducer, names), out_shape...]
    slice x3 -> x0, local copies, waits for them, and re-layouts: 3.63 us -> none  [the longest x1 1.68 us: on_device(): qkv = rest[feat:].astype(F32).reshape(3, feat, width).transpose(2, 0, 1)]
where the time goes in v2:
time: 274 us; the launch traced here: 268 us
  Pallas kernels  267 us (97%)
    pallas_call x1, Pallas kernels, whole_layer(): pl.pallas_call(functools.partial(layer_kernel, reducer, names), out_shape...  257 us
    pallas_call x1, Pallas kernels, finish(): pl.pallas_call(functools.partial(finish_kernel, names), out_shape=tuple(o...  10.7 us

profile of v2, /device:TPU:0, one launch (start us, length us, event | category | flops | bytes accessed | tf_op | source)
XLA Modules:
  0.0 268.4 jit_solution(4893985654205301730)
XLA Ops:
  0.6 256.8 %whole_layer.1 = (bf16[2,2,3360,1120]{3,2,1,0:T(8,128)(2,1)}, bf16[3360,1120]{1,0:T(8,128)(2,1)}, bf16[1120,1120]{1,0:T(8,128)(2,1)}, bf16[1120,1120]{1,0:T(8,12...) custom-call(bf16[4,1120,128]{2,1,0:T(8,128)(2,1)} %bitcast.11, ...), custom_call_target="tpu_custom_call" | custom-call | tf_op jit(solution)/shard_map/whole_layer/pallas_call | solution.py:1053
  257.4 10.7 %finish.1 = (bf16[4,1120,128]{2,1,0:T(8,128)(2,1)}, f32[4,1120,128]{2,1,0:T(8,128)}, f32[840,1120]{1,0:T(8,128)}, f32[280,1120]{1,0:T(8,128)}, f32[1120,1120]{1,...) custom-call(bf16[4,1120,128]{2,1,0:T(8,128)(2,1)} %get-tuple-element, ...), custom_call_target="tpu_custom_call" | custom-call | tf_op jit(solution)/shard_map/finish/pallas_call | solution.py:1156
